TPU v7x, 32 devices: a whole 2x2x4 slice. The times are simulated.
32 devices in a mesh: pipe: 2 (over x), dp: 16 (over z, y, core).
Axes of the slice: x: 2, y: 2, z: 4, core: 2. Of those that a mesh axis runs over, the one named last changes fastest.
Arguments:
- activations: bfloat16 [32, 512, 768], P('dp'), may hold values from -6 to 6
- out_cotangent: bfloat16 [32, 512, 768], P('dp'), may hold values from -6 to 6
- doc_lengths: int32 [32, 5], P('dp'), may hold values from 1 to 256, 512 in all within a row
- mix_gain: float32 [2, 768], P('pipe'), may hold values from 0.25 to 1.75
- mix_bias: float32 [2, 768], P('pipe'), may hold values from -3 to 3
- weight_in: bfloat16 [2, 768, 3072], P('pipe'), may hold values from -0.21875 to 0.21875
- bias_in: float32 [2, 3072], P('pipe'), may hold values from -3 to 3
- weight_out: bfloat16 [2, 3072, 768], P('pipe'), may hold values from -0.109375 to 0.109375
- bias_out: float32 [2, 768], P('pipe'), may hold values from -3 to 3
- final_gain: float32 [2, 768], P('pipe'), may hold values from 0.25 to 1.75
- final_bias: float32 [2, 768], P('pipe'), may hold values from -3 to 3
Outputs:
- layer_outputs: bfloat16 [2, 32, 512, 768], P('pipe', 'dp')
- input_grads: float32 [2, 32, 512, 768], P('pipe', 'dp')
- mix_gain_grad: float32 [2, 768], P('pipe')
- mix_bias_grad: float32 [2, 768], P('pipe')
- weight_in_grad: float32 [2, 768, 3072], P('pipe')
- bias_in_grad: float32 [2, 3072], P('pipe')
- weight_out_grad: float32 [2, 3072, 768], P('pipe')
- bias_out_grad: float32 [2, 768], P('pipe')
- final_gain_grad: float32 [2, 768], P('pipe')
- final_bias_grad: float32 [2, 768], P('pipe')
Inputs may be any that keep to these rules, and one draw needn't show every extreme that they name: `doc_lengths`: in each row the 4 document lengths and, last, the padding's length add up to 512; every row's largest entry is 256.
All inputs are finite; a program needn't handle non-finite values.
Results may differ from a plain program's by a relative error of at most 0.013.
Values may be sent and summed in bfloat16 or wider, within the bound.
No kernel may reach another device: no remote copies, remote signals or barrier semaphores. Data moves between devices by JAX's collectives and lax.ppermute only.
A program may use at most 192 MiB of HBM per device.

v0:
```python
import math

import jax
import jax.numpy as jnp
from jax import lax
from jax.sharding import PartitionSpec as P

MICRO = 2


eps_norm = 1e-06


def from_behind(block, axis, distance):
    devices = range(lax.axis_size(axis))
    route = [(i - distance, i) for i in devices if i - distance in devices]
    return lax.ppermute(block, axis, route)


def dft_tables(table_len):
    indices = jnp.arange(table_len, dtype=jnp.int32)
    product = indices[:, None] * indices[None, :] % table_len
    angles = product.astype(jnp.float32) * (2.0 * math.pi / table_len)
    scaled = 1.0 / math.sqrt(table_len)
    return (jnp.cos(angles) * scaled, jnp.sin(angles) * scaled)


def normalize(values):
    average = jnp.mean(values, axis=-1, keepdims=True)
    centred = values - average
    inverse = lax.rsqrt(jnp.mean(centred * centred, axis=-1, keepdims=True) + eps_norm)
    return (centred * inverse, inverse)


def norm_back(grad_norm, normed, inverse):
    first_term = jnp.mean(grad_norm, axis=-1, keepdims=True)
    second_term = jnp.mean(grad_norm * normed, axis=-1, keepdims=True)
    return inverse * (grad_norm - first_term - normed * second_term)


def gelu_tanh(values):
    return jax.nn.gelu(values, approximate=True)


def forward_parts(layer_in, params, mixers):
    hidden_mix, seq_mix = mixers
    mix_gain, mix_bias, weight_in, bias_in, weight_out, bias_out, final_gain, final_bias = params
    row_count, seq_len, model_width = layer_in.shape
    spectra = jnp.einsum(
        "rld,kde->rkle", layer_in, hidden_mix, preferred_element_type=jnp.float32
    ).astype(jnp.bfloat16)
    stacked_spec = spectra.reshape(row_count, 2 * seq_len, model_width)
    mixed_seq = jnp.einsum("ml,rld->rmd", seq_mix, stacked_spec, preferred_element_type=jnp.float32)
    normed_one, inverse_one = normalize(layer_in.astype(jnp.float32) + mixed_seq)
    hidden = normed_one * mix_gain + mix_bias
    hidden_low = hidden.astype(jnp.bfloat16)
    inner_act = (
        jnp.einsum("rld,df->rlf", hidden_low, weight_in, preferred_element_type=jnp.float32)
        + bias_in
    )
    active = gelu_tanh(inner_act).astype(jnp.bfloat16)
    branch = (
        jnp.einsum("rlf,fd->rld", active, weight_out, preferred_element_type=jnp.float32) + bias_out
    )
    normed_two, inverse_two = normalize(hidden + branch)
    result = normed_two * final_gain + final_bias
    return (
        result,
        (normed_one, inverse_one, hidden_low, inner_act, active, normed_two, inverse_two),
    )


def layer_back(layer_in, grad_out, params, mixers):
    hidden_mix, seq_mix = mixers
    mix_gain, mix_bias, weight_in, bias_in, weight_out, bias_out, final_gain, final_bias = params
    row_count, seq_len, model_width = layer_in.shape
    result, kept_parts = forward_parts(layer_in, params, mixers)
    normed_one, inverse_one, hidden_low, inner_act, active, normed_two, inverse_two = kept_parts
    final_gain_grad = jnp.sum(grad_out * normed_two, axis=(0, 1))
    final_bias_grad = jnp.sum(grad_out, axis=(0, 1))
    grad_sum_two = norm_back(grad_out * final_gain, normed_two, inverse_two)
    grad_branch = grad_sum_two.astype(jnp.bfloat16)
    bias_out_grad = jnp.sum(grad_branch.astype(jnp.float32), axis=(0, 1))
    weight_out_grad = jnp.einsum(
        "rlf,rld->fd", active, grad_branch, preferred_element_type=jnp.float32
    )
    out_side = (weight_out_grad, bias_out_grad, final_gain_grad, final_bias_grad)
    grad_active = jnp.einsum(
        "rld,fd->rlf", grad_branch, weight_out, preferred_element_type=jnp.float32
    )
    unused_value, gelu_pull = jax.vjp(gelu_tanh, inner_act)
    grad_inner = gelu_pull(grad_active)[0].astype(jnp.bfloat16)
    bias_in_grad = jnp.sum(grad_inner.astype(jnp.float32), axis=(0, 1))
    weight_in_grad = jnp.einsum(
        "rld,rlf->df", hidden_low, grad_inner, preferred_element_type=jnp.float32
    )
    grad_hidden = grad_sum_two + jnp.einsum(
        "rlf,df->rld", grad_inner, weight_in, preferred_element_type=jnp.float32
    )
    mix_gain_grad = jnp.sum(grad_hidden * normed_one, axis=(0, 1))
    mix_bias_grad = jnp.sum(grad_hidden, axis=(0, 1))
    grad_mixed = norm_back(grad_hidden * mix_gain, normed_one, inverse_one)
    grad_seq = grad_mixed.astype(jnp.bfloat16)
    grad_spectra = jnp.einsum(
        "ml,rmd->rld", seq_mix, grad_seq, preferred_element_type=jnp.float32
    ).astype(jnp.bfloat16)
    grad_spectra = grad_spectra.reshape(row_count, 2, seq_len, model_width)
    grad_in = grad_mixed + jnp.einsum(
        "rkle,kde->rld", grad_spectra, hidden_mix, preferred_element_type=jnp.float32
    )
    in_side = (mix_gain_grad, mix_bias_grad, weight_in_grad, bias_in_grad)
    return (grad_in, in_side, out_side)


def add_terms(running, addend):
    if running is None:
        return tuple(addend)
    return tuple((first + second for first, second in zip(running, addend)))


def per_device(
    activations,
    out_cotangent,
    doc_lengths,
    mix_gain,
    mix_bias,
    weight_in,
    bias_in,
    weight_out,
    bias_out,
    final_gain,
    final_bias,
):
    is_first = lax.axis_index("pipe") == 0
    row_count, seq_len, model_width = activations.shape
    per_micro = row_count // MICRO
    params = (
        mix_gain[0],
        mix_bias[0],
        weight_in[0],
        bias_in[0],
        weight_out[0],
        bias_out[0],
        final_gain[0],
        final_bias[0],
    )
    cos_hid, sin_hid = dft_tables(model_width)
    cos_seq, sin_seq = dft_tables(seq_len)
    mixers = (
        jnp.stack([cos_hid, sin_hid]).astype(jnp.bfloat16),
        jnp.concatenate([cos_seq, -sin_seq], axis=1).astype(jnp.bfloat16),
    )
    padding = doc_lengths[:, -1]
    positions = jnp.arange(seq_len, dtype=jnp.int32)
    token_mask = (positions[None, :] < (seq_len - padding)[:, None]).astype(jnp.float32)
    cotangent = out_cotangent.astype(jnp.float32) * token_mask[:, :, None]
    empty_in = jnp.zeros((per_micro, seq_len, model_width), jnp.bfloat16)
    empty_grad = jnp.zeros((per_micro, seq_len, model_width), jnp.float32)
    received = empty_in
    section_inputs = []
    section_outputs = []
    for moment in range(MICRO + 1):
        own_rows = (
            activations[moment * per_micro : (moment + 1) * per_micro]
            if moment < MICRO
            else empty_in
        )
        current = jnp.where(is_first, own_rows, received)
        result, kept_parts = forward_parts(current, params, mixers)
        sent_low = result.astype(jnp.bfloat16)
        section_inputs.append(current)
        section_outputs.append(sent_low)
        if moment < MICRO:
            received = from_behind(sent_low, "pipe", 1)
    grad_received = empty_in
    grad_inputs = []
    totals_in = None
    totals_out = None
    for moment in range(MICRO + 1):
        earlier = section_inputs[moment - 1] if moment >= 1 else empty_in
        later_input = section_inputs[moment + 1] if moment < MICRO else empty_in
        current = jnp.where(is_first, earlier, later_input)
        own_grad = (
            cotangent[moment * per_micro : (moment + 1) * per_micro]
            if moment < MICRO
            else empty_grad
        )
        grad_out = jnp.where(is_first, grad_received.astype(jnp.float32), own_grad)
        grad_in, in_terms, out_terms = layer_back(current, grad_out, params, mixers)
        totals_out = add_terms(totals_out, out_terms)
        totals_in = add_terms(totals_in, in_terms)
        grad_low = grad_in.astype(jnp.bfloat16)
        grad_inputs.append(jnp.where(is_first, grad_in, grad_low.astype(jnp.float32)))
        if moment < MICRO:
            grad_received = from_behind(grad_low, "pipe", -1)
    ordered = (
        totals_in[0],
        totals_in[1],
        totals_in[2],
        totals_in[3],
        totals_out[0],
        totals_out[1],
        totals_out[2],
        totals_out[3],
    )
    totals = lax.psum(
        (
            ordered[0],
            ordered[1],
            ordered[2],
            ordered[3],
            ordered[4],
            ordered[5],
            ordered[6],
            ordered[7],
        ),
        "dp",
    )
    layer_rows = jnp.concatenate(
        [
            jnp.where(is_first, section_outputs[index_m], section_outputs[index_m + 1])
            for index_m in range(MICRO)
        ],
        axis=0,
    )
    grad_rows = jnp.concatenate(
        [
            jnp.where(is_first, grad_inputs[index_m + 1], grad_inputs[index_m])
            for index_m in range(MICRO)
        ],
        axis=0,
    )
    return (
        layer_rows[None],
        grad_rows[None],
        totals[0][None],
        totals[1][None],
        totals[2][None],
        totals[3][None],
        totals[4][None],
        totals[5][None],
        totals[6][None],
        totals[7][None],
    )


def solution(mesh):
    placed = (
        P("dp", None, None),
        P("dp", None, None),
        P("dp", None),
        P("pipe", None),
        P("pipe", None),
        P("pipe", None, None),
        P("pipe", None),
        P("pipe", None, None),
        P("pipe", None),
        P("pipe", None),
        P("pipe", None),
    )
    return jax.shard_map(
        per_device,
        mesh=mesh,
        in_specs=placed,
        out_specs=(
            P("pipe", "dp", None, None),
            P("pipe", "dp", None, None),
            P("pipe", None),
            P("pipe", None),
            P("pipe", None, None),
            P("pipe", None),
            P("pipe", None, None),
            P("pipe", None),
            P("pipe", None),
            P("pipe", None),
        ),
        check_vma=False,
    )
```

profile of v0, /device:TPU:0, one launch (start us, length us, event | category | flops | bytes accessed | tf_op | source)
XLA Modules:
  0.0 591.6 jit_solution(8047918946627711519)
XLA Ops:
  7.2 10.0 %multiply_convert_fusion.3 = (bf16[1,768,768]{2,1,0:T(8,128)(2,1)S(1)}, bf16[1,768,768]{2,1,0:T(8,128)(2,1)S(1)}) fusion(), kind=kLoop, calls=%fused_computation.104 | loop fusion | flops 7667712 | bytes 2359296 | tf_op jit(solution)/shard_map/convert.3
  17.3 5.6 negate_convert_fusion
  22.9 2.7 convolution_convert_fusion.8
  27.4 6.9 %fusion.28 = bf16[512,3072]{1,0:T(8,128)(2,1)S(1)} fusion(bf16[1,768,3072]{2,1,0:T(8,128)(2,1)} %param.16, f32[3072]{0:T(1024)S(1)} %bitcast.301, f32[1,512,768]{2,1,0:T(8,128)S(1)} %get-tuple-element.54, f32[768]{0:T(1024)S(1)} %reduce.43, f32[768]{0:T(1024)S(1)} %reduce.42, f32[512]{0:T(512)S(1)} %add_rsqrt_fusion.11, f32[512]{0:T(512)S(1)} %broadcast_multiply_fusion.23), kind=kOutput, calls=%fused_computation.39 | convolution fusion | flops 2433613824 | bytes 9459712 | tf_op jit(solution)/shard_map/rld,df->rlf/dot_general | solution.py:58
  34.3 5.1 fusion.201
  40.5 5.1 collective-permute-start
  45.9 1.9 convert_multiply_fusion
  47.9 14.3 %collective-permute-done = bf16[1,512,768]{2,1,0:T(8,128)(2,1)S(1)} collective-permute-done((bf16[1,512,768]{2,1,0:T(8,128)(2,1)S(1)}, bf16[1,512,768]{2,1,0:T(8,128)(2,1)S(1)}, u32[]{:S(2)}, u32[]{:S(2)}) %collective-permute-start) | collective-permute-done | bytes 786464 | tf_op jit(solution)/shard_map/ppermute | solution.py:17
  65.1 2.5 convolution_convert_fusion.3
  70.5 2.7 fusion.71
  73.3 4.2 fusion.209
  80.3 7.5 %convert_reduce_fusion.2 = (f32[3072]{0:T(1024)}, bf16[512,3072]{1,0:T(8,128)(2,1)S(1)}) fusion(f32[512,3072]{1,0:T(8,128)S(1)} %fusion.71, f32[3072]{0:T(1024)S(1)} %bitcast.303, bf16[1,3072,768]{2,1,0:T(8,128)(2,1)S(1)} %bitcast.314, f32[1,512,768]{2,1,0:T(8,128)S(1)} %get-tuple-element.45), kind=kOutput, calls=%fused_computation.58 | convolution fusion | flops 2452485120 | bytes 15753216 | tf_op jit(solution)/shard_map/rld,fd->rlf/dot_general | solution.py:88
  87.8 3.6 multiply_reduce_fusion.5
  91.4 5.5 fusion.195
  98.3 4.8 fusion.36
  103.2 2.8 fusion.203
  107.4 1.8 broadcast_select_fusion.4
  109.2 5.3 collective-permute-start.1
  114.5 2.5 fusion.107
  117.0 2.6 copy.36
  119.6 5.8 fusion.210
  128.2 5.5 fusion.65
  133.8 4.2 fusion.212
  140.0 6.6 %fusion.154 = f32[3072,768]{1,0:T(8,128)} fusion(f32[1,512,768]{2,1,0:T(8,128)S(1)} %copy-done.12, f32[512,3072]{1,0:T(8,128)S(1)} %bitcast.334, f32[3072]{0:T(1024)S(1)} %bitcast.306), kind=kOutput, calls=%fused_computation.238 | convolution fusion | flops 2432040960 | bytes 17313792 | tf_op jit(solution)/shard_map/rlf,rld->fd/dot_general | solution.py:84
  150.9 2.7 fusion.73
  153.7 4.2 fusion.207
  159.7 6.8 %convert_reduce_fusion.1 = (f32[3072]{0:T(1024)S(1)}, bf16[512,3072]{1,0:T(8,128)(2,1)S(1)}) fusion(f32[512,3072]{1,0:T(8,128)S(1)} %fusion.73, f32[3072]{0:T(1024)S(1)} %bitcast.308, bf16[1,3072,768]{2,1,0:T(8,128)(2,1)S(1)} %bitcast.316, f32[1,512,768]{2,1,0:T(8,128)S(1)} %get-tuple-element.43), kind=kOutput, calls=%fused_computation.57 | convolution fusion | flops 2452485120 | bytes 15753216 | tf_op jit(solution)/shard_map/rld,fd->rlf/dot_general | solution.py:88
  166.5 3.2 multiply_reduce_fusion.4
  169.7 5.5 fusion.192
  175.2 2.6 fusion.108
  177.8 1.8 copy.37
  179.7 6.3 %select_select_fusion.1 = (f32[1,512,768]{2,1,0:T(8,128)}, bf16[1,512,768]{2,1,0:T(8,128)(2,1)S(1)}, f32[1,512,768]{2,1,0:T(8,128)}) fusion(f32[1,512,768]{2,1,0:T(8,128)} %get-tuple-element.75, bf16[1,512,768]{2,1,0:T(8,128)(2,1)} %copy-done.50, pred[]{:T(512)S(6)} %eq.7, bf16[2,512,768]{2,1,0:T(8,128)(2,1)S(1)} %bitcast.298, ...), kind=kOutput, calls=%fused_computation.161 | convolution fusion | flops 1214644224 | bytes 13380609 | tf_op jit(solution)/shard_map/rkle,kde->rld/dot_general | solution.py:108
  187.6 10.3 %fusion.150 = f32[3072,768]{1,0:T(8,128)} fusion(f32[1,512,768]{2,1,0:T(8,128)S(1)} %copy-done.18, f32[512,3072]{1,0:T(8,128)} %copy-done.54, f32[3072]{0:T(1024)S(1)} %bitcast.309), kind=kOutput, calls=%fused_computation.234 | convolution fusion | flops 2432040960 | bytes 17313792 | tf_op jit(solution)/shard_map/rlf,rld->fd/dot_general | solution.py:84
  197.9 9.0 %collective-permute-done.3 = bf16[1,512,768]{2,1,0:T(8,128)(2,1)S(1)} collective-permute-done((bf16[1,512,768]{2,1,0:T(8,128)(2,1)S(1)}, bf16[1,512,768]{2,1,0:T(8,128)(2,1)S(1)}, u32[]{:S(2)}, u32[]{:S(2)}) %collective-permute-start.3) | collective-permute-done | bytes 786464 | tf_op jit(solution)/shard_map/ppermute | solution.py:17
  208.5 6.8 %convert_reduce_fusion = (f32[3072]{0:T(1024)S(1)}, bf16[512,3072]{1,0:T(8,128)(2,1)S(1)}) fusion(f32[512,3072]{1,0:T(8,128)S(1)} %bitcast.296, f32[3072]{0:T(1024)S(1)} %bitcast.310, bf16[1,3072,768]{2,1,0:T(8,128)(2,1)S(1)} %bitcast.318, f32[1,512,768]{2,1,0:T(8,128)S(1)} %get-tuple-element.47), kind=kOutput, calls=%fused_computation.56 | convolution fusion | flops 2452485120 | bytes 15753216 | tf_op jit(solution)/shard_map/rld,fd->rlf/dot_general | solution.py:88
  215.3 17.0 %add_bitcast_fusion = f32[1,3072,768]{2,1,0:T(8,128)} fusion(f32[3072,768]{1,0:T(8,128)} %fusion.154, f32[3072,768]{1,0:T(8,128)} %fusion.150, f32[1,512,768]{2,1,0:T(8,128)S(1)} %get-tuple-element.47, f32[512,3072]{1,0:T(8,128)} %copy-done.7, f32[3072]{0:T(1024)S(1)} %bitcast.311), kind=kOutput, calls=%fused_computation.3 | convolution fusion | flops 2436759552 | bytes 36188160 | tf_op jit(solution)/shard_map/rlf,rld->fd/dot_general | solution.py:84
  232.4 8.4 %add_bitcast_fusion.1 = f32[1,768,3072]{2,1,0:T(8,128)} fusion(f32[768,3072]{1,0:T(8,128)S(1)} %bitcast.294, f32[768,3072]{1,0:T(8,128)} %fusion.192, bf16[512,3072]{1,0:T(8,128)(2,1)S(1)} %get-tuple-element.84, f32[1,512,768]{2,1,0:T(8,128)S(1)} %copy-done.6, f32[512]{0:T(512)S(1)} %add_rsqrt_fusion.1, f32[512]{0:T(512)S(1)} %broadcast_multiply_fusion.5, ...), kind=kOutput, calls=%fused_computation.4 | convolution fusion | flops 2422603776 | bytes 33040384 | tf_op jit(solution)/shard_map/rld,rlf->df/dot_general | solution.py:94
  240.8 3.1 convolution_convert_fusion.6
  245.3 8.4 %fusion.44 = bf16[512,3072]{1,0:T(8,128)(2,1)S(1)} fusion(bf16[1,768,3072]{2,1,0:T(8,128)(2,1)} %param.16, f32[3072]{0:T(1024)S(1)} %bitcast.312, f32[1,512,768]{2,1,0:T(8,128)S(1)} %get-tuple-element.62, f32[512]{0:T(512)S(1)} %add_rsqrt_fusion.7, f32[512]{0:T(512)S(1)} %broadcast_multiply_fusion.19, f32[768]{0:T(1024)S(1)} %reduce.43, f32[768]{0:T(1024)S(1)} %reduce.42), kind=kOutput, calls=%fused_computation.55 | convolution fusion | flops 2433613824 | bytes 9459712 | tf_op jit(solution)/shard_map/rld,df->rlf/dot_general | solution.py:58
  253.8 2.8 fusion.205
  261.1 3.1 multiply_reduce_fusion.3
  265.4 2.5 fusion.109
  269.6 62.0 %all-reduce = (f32[1,768]{1,0:T(1,128)}, f32[1,768]{1,0:T(1,128)}, f32[1,3072]{1,0:T(1,128)}, f32[1,768]{1,0:T(1,128)}, f32[1,768]{1,0:T(1,128)}, /*index=5*/f32[1,768]{1,0:T(1,128)}) all-reduce(f32[1,768]{1,0:T(1,128)S(1)} %broadcast_in_dim.28, f32[1,768]{1,0:T(1,128)S(1)} %broadcast_in_dim.29, ...), channel_id=1, replica_groups=mesh['pipe'=2,'dp'=16] {'dp'}, use_global_device_ids=true, to_apply=%region_39.40 | all-reduce | flops 6912 | bytes 55296 | tf_op jit(solution)/shard_map/psum | solution.py:206
  331.7 4.9 select_select_fusion
  336.6 1.9 maximum_bitcast_fusion
  338.4 233.4 %all-reduce.4.cloned.1.call-done = (f32[1,768,3072]{2,1,0:T(8,128)}, f32[1,3072,768]{2,1,0:T(8,128)}) async-done(((f32[1,768,3072]{2,1,0:T(8,128)}, f32[1,3072,768]{2,1,0:T(8,128)}), (f32[1,768,3072]{2,1,0:T(8,128)}, f32[1,3072,768]{2,1,0:T(8,128)})) %all-reduce.4.cloned.1.call-update) | async-done | bytes 18874384 | tf_op jit(solution)/shard_map/psum | solution.py:206
  571.8 8.8 %copy.41 = f32[1,768,3072]{2,1,0:T(8,128)} copy(f32[1,768,3072]{2,1,0:T(8,128)} %get-tuple-element.97) | data formatting | bytes 18874368
  580.5 3.7 copy.42
  (260 shorter events, 36.9 us)
Async XLA Ops:
  7.2 564.6 %all-reduce.4.cloned.1.call-start = ((), (), s32[]{:S(2)}) async-start(), calls=%async_computation | async-start | bytes 37748736 | tf_op jit(solution)/shard_map/psum | solution.py:206
  17.3 8.3 %copy-start.19 = (bf16[1,768,768]{2,1,0:T(8,128)(2,1)}, bf16[1,768,768]{2,1,0:T(8,128)(2,1)S(1)}, u32[]{:S(2)}) copy-start(bf16[1,768,768]{2,1,0:T(8,128)(2,1)S(1)} %get-tuple-element.89) | copy-start | bytes 3538948
  17.3 8.3 %copy-start.22 = (bf16[1,768,768]{2,1,0:T(8,128)(2,1)}, bf16[1,768,768]{2,1,0:T(8,128)(2,1)S(1)}, u32[]{:S(2)}) copy-start(bf16[1,768,768]{2,1,0:T(8,128)(2,1)S(1)} %get-tuple-element.90) | copy-start | bytes 3538948
  39.7 5.9 copy-start.51
  40.5 21.6 %collective-permute-start = (bf16[1,512,768]{2,1,0:T(8,128)(2,1)S(1)}, bf16[1,512,768]{2,1,0:T(8,128)(2,1)S(1)}, u32[]{:S(2)}, u32[]{:S(2)}) collective-permute-start(bf16[1,512,768]{2,1,0:T(8,128)(2,1)S(1)} %add_convert_fusion.2), channel_id=1, source_target_pairs={{0,16},{1,17},{2,18},{3,19},{4,20},{5,21},{6,22},{7,23},{8,24},{9,... | collective-permute-start | bytes 2359304 | tf_op jit(solution)/shard_map/ppermute | solution.py:17
  45.9 16.3 %copy-start.36 = (bf16[2,512,768]{2,1,0:T(8,128)(2,1)S(1)}, bf16[2,512,768]{2,1,0:T(8,128)(2,1)}, u32[]{:S(2)}) copy-start(bf16[2,512,768]{2,1,0:T(8,128)(2,1)} %param.11) | copy-start | bytes 4718596
  47.8 14.4 %copy-start.20 = (bf16[1,768,768]{2,1,0:T(8,128)(2,1)S(1)}, bf16[1,768,768]{2,1,0:T(8,128)(2,1)}, u32[]{:S(2)}) copy-start(bf16[1,768,768]{2,1,0:T(8,128)(2,1)} %copy-done.19) | copy-start | bytes 3538948
  47.8 14.4 %copy-start.23 = (bf16[1,768,768]{2,1,0:T(8,128)(2,1)S(1)}, bf16[1,768,768]{2,1,0:T(8,128)(2,1)}, u32[]{:S(2)}) copy-start(bf16[1,768,768]{2,1,0:T(8,128)(2,1)} %copy-done.22) | copy-start | bytes 3538948
  62.3 34.7 %copy-start.25 = (bf16[1,512,768]{2,1,0:T(8,128)(2,1)}, bf16[1,512,768]{2,1,0:T(8,128)(2,1)S(1)}, u32[]{:S(2)}) copy-start(bf16[1,512,768]{2,1,0:T(8,128)(2,1)S(1)} %slice_select_fusion.2) | copy-start | bytes 2359300
  68.7 45.8 %copy-start.13 = (f32[1,512,768]{2,1,0:T(8,128)}, f32[1,512,768]{2,1,0:T(8,128)S(1)}, u32[]{:S(2)}) copy-start(f32[1,512,768]{2,1,0:T(8,128)S(1)} %get-tuple-element.70) | copy-start | bytes 4718596
  73.3 7.0 %copy-start.53 = (f32[512,3072]{1,0:T(8,128)}, f32[512,3072]{1,0:T(8,128)S(1)}, u32[]{:S(2)}) copy-start(f32[512,3072]{1,0:T(8,128)S(1)} %fusion.71) | copy-start | bytes 18874372
  80.3 7.5 %copy-start.11 = (f32[1,512,768]{2,1,0:T(8,128)}, f32[1,512,768]{2,1,0:T(8,128)S(1)}, u32[]{:S(2)}) copy-start(f32[1,512,768]{2,1,0:T(8,128)S(1)} %get-tuple-element.45) | copy-start | bytes 4718596
  91.4 23.1 %copy-start.56 = (f32[1,512,768]{2,1,0:T(8,128)}, f32[1,512,768]{2,1,0:T(8,128)S(1)}, u32[]{:S(2)}) copy-start(f32[1,512,768]{2,1,0:T(8,128)S(1)} %get-tuple-element.73) | copy-start | bytes 4718596
  109.2 37.4 %collective-permute-start.1 = (bf16[1,512,768]{2,1,0:T(8,128)(2,1)}, bf16[1,512,768]{2,1,0:T(8,128)(2,1)}, u32[]{:S(2)}, u32[]{:S(2)}) collective-permute-start(bf16[1,512,768]{2,1,0:T(8,128)(2,1)} %get-tuple-element.50), channel_id=1, source_target_pairs={{0,16},{1,17},{2,18},{3,19},{4,20},{5,21},{6,22},{7,23},{8,24},{9,... | collective-permute-start | bytes 2359304 | tf_op jit(solution)/shard_map/ppermute | solution.py:17
  119.6 7.1 %copy-start.26 = (bf16[1,512,768]{2,1,0:T(8,128)(2,1)S(1)}, bf16[1,512,768]{2,1,0:T(8,128)(2,1)}, u32[]{:S(2)}) copy-start(bf16[1,512,768]{2,1,0:T(8,128)(2,1)} %copy-done.25) | copy-start | bytes 2359300
  119.6 7.1 %copy-start.29 = (bf16[512,512]{1,0:T(8,128)(2,1)S(1)}, bf16[512,512]{1,0:T(8,128)(2,1)}, u32[]{:S(2)}) copy-start(bf16[512,512]{1,0:T(8,128)(2,1)} %get-tuple-element.91) | copy-start | bytes 1572868
  119.6 7.2 %copy-start.33 = (bf16[512,512]{1,0:T(8,128)(2,1)S(1)}, bf16[512,512]{1,0:T(8,128)(2,1)}, u32[]{:S(2)}) copy-start(bf16[512,512]{1,0:T(8,128)(2,1)} %get-tuple-element.92) | copy-start | bytes 1572868
  119.6 7.2 %copy-start.52 = (bf16[2,768,512]{1,2,0:T(8,128)(2,1)S(1)}, bf16[2,768,512]{1,2,0:T(8,128)(2,1)}, u32[]{:S(2)}) copy-start(bf16[2,768,512]{1,2,0:T(8,128)(2,1)} %convolution_convert_fusion.3) | copy-start | bytes 4718596
  125.5 32.8 %collective-permute-start.2 = (bf16[1,512,768]{2,1,0:T(8,128)(2,1)S(1)}, bf16[1,512,768]{2,1,0:T(8,128)(2,1)S(1)}, u32[]{:S(2)}, u32[]{:S(2)}) collective-permute-start(bf16[1,512,768]{2,1,0:T(8,128)(2,1)S(1)} %get-tuple-element.74), channel_id=1, source_target_pairs={{16,0},{17,1},{18,2},{19,3},{20,4},{21,5},{22,6},{23,7},{24,8},{25... | collective-permute-start | bytes 2359304 | tf_op jit(solution)/shard_map/ppermute | solution.py:17
  126.8 6.9 %slice-start.7 = ((s8[4718592]{0:T(1024)(128)(4,1)}), s8[4194304]{0:T(1024)(128)(4,1)S(1)}, s32[]{:S(2)}) async-start(s8[4718592]{0:T(1024)(128)(4,1)} %bitcast.315), calls=%async_computation.8 | async-start | bytes 8388608
  127.9 5.8 copy-start.5
  128.2 11.3 %slice-start.19 = ((s8[6291456]{0:T(1024)(128)(4,1)}), s8[4194304]{0:T(1024)(128)(4,1)S(1)}, s32[]{:S(2)}) async-start(s8[6291456]{0:T(1024)(128)(4,1)} %bitcast.333), calls=%async_computation.20 | async-start | bytes 8388608
  133.7 5.7 slice-start.20
  140.0 6.7 %copy-start.21 = (bf16[1,768,768]{2,1,0:T(8,128)(2,1)S(1)}, bf16[1,768,768]{2,1,0:T(8,128)(2,1)}, u32[]{:S(2)}) copy-start(bf16[1,768,768]{2,1,0:T(8,128)(2,1)} %copy-done.19) | copy-start | bytes 3538948
  140.0 6.7 %copy-start.24 = (bf16[1,768,768]{2,1,0:T(8,128)(2,1)S(1)}, bf16[1,768,768]{2,1,0:T(8,128)(2,1)}, u32[]{:S(2)}) copy-start(bf16[1,768,768]{2,1,0:T(8,128)(2,1)} %copy-done.22) | copy-start | bytes 3538948
  140.0 6.7 %copy-start.37 = (bf16[2,512,768]{2,1,0:T(8,128)(2,1)S(1)}, bf16[2,512,768]{2,1,0:T(8,128)(2,1)}, u32[]{:S(2)}) copy-start(bf16[2,512,768]{2,1,0:T(8,128)(2,1)} %param.11) | copy-start | bytes 4718596
  149.2 26.0 %copy-start.14 = (f32[1,512,768]{2,1,0:T(8,128)}, f32[1,512,768]{2,1,0:T(8,128)S(1)}, u32[]{:S(2)}) copy-start(f32[1,512,768]{2,1,0:T(8,128)S(1)} %get-tuple-element.66) | copy-start | bytes 4718596
  153.7 6.0 %copy-start.54 = (f32[512,3072]{1,0:T(8,128)}, f32[512,3072]{1,0:T(8,128)S(1)}, u32[]{:S(2)}) copy-start(f32[512,3072]{1,0:T(8,128)S(1)} %fusion.73) | copy-start | bytes 18874372
  159.7 6.8 %copy-start.17 = (f32[1,512,768]{2,1,0:T(8,128)}, f32[1,512,768]{2,1,0:T(8,128)S(1)}, u32[]{:S(2)}) copy-start(f32[1,512,768]{2,1,0:T(8,128)S(1)} %get-tuple-element.43) | copy-start | bytes 4718596
  169.7 5.6 copy-start.55
  179.7 7.9 %copy-start.18 = (f32[1,512,768]{2,1,0:T(8,128)S(1)}, f32[1,512,768]{2,1,0:T(8,128)}, u32[]{:S(2)}) copy-start(f32[1,512,768]{2,1,0:T(8,128)} %copy-done.17) | copy-start | bytes 4718596
  179.7 28.7 %slice-start.3 = ((s8[6291456]{0:T(1024)(128)(4,1)}), s8[4194304]{0:T(1024)(128)(4,1)S(1)}, s32[]{:S(2)}) async-start(s8[6291456]{0:T(1024)(128)(4,1)} %bitcast.295), calls=%async_computation.4 | async-start | bytes 8388608
  179.7 28.7 %slice-start.9 = ((s8[4718592]{0:T(1024)(128)(4,1)}), s8[4194304]{0:T(1024)(128)(4,1)S(1)}, s32[]{:S(2)}) async-start(s8[4718592]{0:T(1024)(128)(4,1)} %bitcast.317), calls=%async_computation.10 | async-start | bytes 8388608
  186.0 20.9 %copy-start.3 = (f32[1,512,768]{2,1,0:T(8,128)S(1)}, f32[1,512,768]{2,1,0:T(8,128)}, u32[]{:S(2)}) copy-start(f32[1,512,768]{2,1,0:T(8,128)} %copy-done.2) | copy-start | bytes 4718596
  186.0 22.4 %slice-start.4 = ((s8[6291456]{0:T(1024)(128)(4,1)}), s8[2097152]{0:T(1024)(128)(4,1)S(1)}, s32[]{:S(2)}) async-start(s8[6291456]{0:T(1024)(128)(4,1)} %bitcast.295), calls=%async_computation.5 | async-start | bytes 4194304
  186.0 22.4 %slice-start.10 = ((s8[4718592]{0:T(1024)(128)(4,1)}), s8[524288]{0:T(1024)(128)(4,1)S(1)}, s32[]{:S(2)}) async-start(s8[4718592]{0:T(1024)(128)(4,1)} %bitcast.317), calls=%async_computation.11 | async-start | bytes 1048576
  186.0 20.9 %collective-permute-start.3 = (bf16[1,512,768]{2,1,0:T(8,128)(2,1)S(1)}, bf16[1,512,768]{2,1,0:T(8,128)(2,1)S(1)}, u32[]{:S(2)}, u32[]{:S(2)}) collective-permute-start(bf16[1,512,768]{2,1,0:T(8,128)(2,1)S(1)} %get-tuple-element.52), channel_id=1, source_target_pairs={{16,0},{17,1},{18,2},{19,3},{20,4},{21,5},{22,6},{23,7},{24,8},{25... | collective-permute-start | bytes 2359304 | tf_op jit(solution)/shard_map/ppermute | solution.py:17
  208.4 23.9 %slice-start = ((s8[9437184]{0:T(1024)(128)(4,1)}), s8[4194304]{0:T(1024)(128)(4,1)S(1)}, s32[]{:S(2)}) async-start(s8[9437184]{0:T(1024)(128)(4,1)} %bitcast.293), calls=%async_computation.1 | async-start | bytes 8388608
  208.5 23.9 %slice-start.1 = ((s8[9437184]{0:T(1024)(128)(4,1)}), s8[4194304]{0:T(1024)(128)(4,1)S(1)}, s32[]{:S(2)}) async-start(s8[9437184]{0:T(1024)(128)(4,1)} %bitcast.293), calls=%async_computation.2 | async-start | bytes 8388608
  215.3 17.1 %copy-start.8 = (bf16[512,3072]{1,0:T(8,128)(2,1)}, bf16[512,3072]{1,0:T(8,128)(2,1)S(1)}, u32[]{:S(2)}) copy-start(bf16[512,3072]{1,0:T(8,128)(2,1)S(1)} %get-tuple-element.84) | copy-start | bytes 9437188
  215.3 17.1 %slice-start.2 = ((s8[9437184]{0:T(1024)(128)(4,1)}), s8[1048576]{0:T(1024)(128)(4,1)S(1)}, s32[]{:S(2)}) async-start(s8[9437184]{0:T(1024)(128)(4,1)} %bitcast.293), calls=%async_computation.3 | async-start | bytes 2097152
  215.3 17.1 %copy-start.6 = (f32[1,512,768]{2,1,0:T(8,128)S(1)}, f32[1,512,768]{2,1,0:T(8,128)}, u32[]{:S(2)}) copy-start(f32[1,512,768]{2,1,0:T(8,128)} %copy-done.5) | copy-start | bytes 4718596
  243.9 9.9 %slice-start.11 = ((s8[4718592]{0:T(1024)(128)(4,1)}), s8[4194304]{0:T(1024)(128)(4,1)S(1)}, s32[]{:S(2)}) async-start(s8[4718592]{0:T(1024)(128)(4,1)} %bitcast.319), calls=%async_computation.12 | async-start | bytes 8388608
  245.3 8.5 %slice-start.12 = ((s8[4718592]{0:T(1024)(128)(4,1)}), s8[524288]{0:T(1024)(128)(4,1)S(1)}, s32[]{:S(2)}) async-start(s8[4718592]{0:T(1024)(128)(4,1)} %bitcast.319), calls=%async_computation.13 | async-start | bytes 1048576
  245.3 14.7 %slice-start.17 = ((s8[4718592]{0:T(1024)(128)(4,1)}), s8[4194304]{0:T(1024)(128)(4,1)S(1)}, s32[]{:S(2)}) async-start(s8[4718592]{0:T(1024)(128)(4,1)} %bitcast.325), calls=%async_computation.18 | async-start | bytes 8388608
  253.8 6.1 %copy-start.40 = (f32[768]{0:T(1024)S(1)}, f32[768]{0:T(1024)}, u32[]{:S(2)}) copy-start(f32[768]{0:T(1024)} %get-tuple-element.21) | copy-start | bytes 9220
  253.8 6.2 %slice-start.18 = ((s8[4718592]{0:T(1024)(128)(4,1)}), s8[524288]{0:T(1024)(128)(4,1)S(1)}, s32[]{:S(2)}) async-start(s8[4718592]{0:T(1024)(128)(4,1)} %bitcast.325), calls=%async_computation.19 | async-start | bytes 1048576
  571.8 8.8 %copy-start.4 = (f32[1,3072,768]{2,1,0:T(8,128)S(1)}, f32[1,3072,768]{2,1,0:T(8,128)}, u32[]{:S(2)}) copy-start(f32[1,3072,768]{2,1,0:T(8,128)} %get-tuple-element.99) | copy-start | bytes 28311556
  (36 other events, 82.5 us)
Sparse Core Ops, SparseCore 0:
  240.9 330.8 all-reduce.3
where the time goes:
time: 599 us; the launch traced here: 592 us
  waiting for transfers between devices  257 us (43%)
  matrix products  182 us (30%)
  blocking collectives  62 us (10%)
  other arithmetic  34 us (6%)
  local copies, waits for them, and re-layouts  27.5 us (5%)
  between operations  15.8 us (3%)
  starting transfers between devices  13.3 us (2%)
    psum x1, waiting for transfers between devices, per_device(): lax.psum((ordered[0], ordered[1], ordered[2], ordered[3], ordered[4], ord...  233 us
    psum x1, blocking collectives, per_device(): lax.psum((ordered[0], ordered[1], ordered[2], ordered[3], ordered[4], ord...  62 us
    dot_general x3, matrix products, layer_back(): jnp.einsum('rlf,rld->fd', active, grad_branch, preferred_element_type=jnp...  34 us
    dot_general x6, matrix products, forward_parts(): jnp.einsum('rld,df->rlf', hidden_low, weight_in, preferred_element_type=j...  31 us
    ppermute x4, waiting for transfers between devices, from_behind(): return lax.ppermute(block, axis, route)  23.3 us
    dot_general x6, matrix products, forward_parts(): jnp.einsum('rlf,fd->rld', active, weight_out, preferred_element_type=jnp....  23.3 us
    unnamed x160, local copies, waits for them, and re-layouts  21.3 us
    dot_general x3, matrix products, layer_back(): jnp.einsum('rld,fd->rlf', grad_branch, weight_out, preferred_element_type...  21.1 us
  transfers between devices with their start and end apart: 5, of which 3 were waited for; matrix products, arithmetic and copies ran while one was open for 14% of the time, Pallas kernels for 0%

commit v1 on v0

v1 whole, which is shorter than its diff:
```python
import functools
import math

import jax
import jax.numpy as jnp
import numpy as np
from jax import lax
from jax.sharding import PartitionSpec as P


eps_norm = 1e-06


def from_behind(block, axis, distance):
    devices = range(lax.axis_size(axis))
    route = [(i - distance, i) for i in devices if i - distance in devices]
    return lax.ppermute(block, axis, route)


def dft_tables(table_len):
    indices = np.arange(table_len)
    angles = (indices[:, None] * indices[None, :] % table_len) * (2.0 * math.pi / table_len)
    scaled = 1.0 / math.sqrt(table_len)
    return (np.cos(angles) * scaled, np.sin(angles) * scaled)


def normalize(values):
    average = jnp.mean(values, axis=-1, keepdims=True)
    centred = values - average
    inverse = lax.rsqrt(jnp.mean(centred * centred, axis=-1, keepdims=True) + eps_norm)
    return (centred * inverse, inverse)


def norm_back(grad_norm, normed, inverse):
    first_term = jnp.mean(grad_norm, axis=-1, keepdims=True)
    second_term = jnp.mean(grad_norm * normed, axis=-1, keepdims=True)
    return inverse * (grad_norm - first_term - normed * second_term)


def gelu_tanh(values):
    return jax.nn.gelu(values, approximate=True)


def forward_parts(layer_in, params, mixers):
    hidden_mix, seq_mix = mixers
    mix_gain, mix_bias, weight_in, bias_in, weight_out, bias_out, final_gain, final_bias = params
    row_count, seq_len, model_width = layer_in.shape
    spectra = jnp.einsum(
        "rld,kde->rkle", layer_in, hidden_mix, preferred_element_type=jnp.float32
    ).astype(jnp.bfloat16)
    stacked_spec = spectra.reshape(row_count, 2 * seq_len, model_width)
    mixed_seq = jnp.einsum("ml,rld->rmd", seq_mix, stacked_spec, preferred_element_type=jnp.float32)
    normed_one, inverse_one = normalize(layer_in.astype(jnp.float32) + mixed_seq)
    hidden = normed_one * mix_gain + mix_bias
    hidden_low = hidden.astype(jnp.bfloat16)
    inner_act = (
        jnp.einsum("rld,df->rlf", hidden_low, weight_in, preferred_element_type=jnp.float32)
        + bias_in
    )
    active = gelu_tanh(inner_act).astype(jnp.bfloat16)
    branch = (
        jnp.einsum("rlf,fd->rld", active, weight_out, preferred_element_type=jnp.float32) + bias_out
    )
    normed_two, inverse_two = normalize(hidden + branch)
    result = normed_two * final_gain + final_bias
    return (
        result,
        (normed_one, inverse_one, hidden_low, inner_act, active, normed_two, inverse_two),
    )


def back_branch(grad_out, kept_parts, params):
    final_gain = params[6]
    normed_two, inverse_two = kept_parts[5:]
    final_gain_grad = jnp.sum(grad_out * normed_two, axis=0)
    final_bias_grad = jnp.sum(grad_out, axis=0)
    grad_sum_two = norm_back(grad_out * final_gain, normed_two, inverse_two)
    grad_branch = grad_sum_two.astype(jnp.bfloat16)
    bias_out_grad = jnp.sum(grad_branch.astype(jnp.float32), axis=0)
    return (grad_sum_two, grad_branch, (bias_out_grad, final_gain_grad, final_bias_grad))


def back_inner(grad_branch, kept_parts, params):
    weight_out, inner_act = (params[4], kept_parts[3])
    grad_active = jnp.einsum("ld,fd->lf", grad_branch, weight_out, preferred_element_type=jnp.float32)
    unused_value, gelu_pull = jax.vjp(gelu_tanh, inner_act)
    grad_inner = gelu_pull(grad_active)[0].astype(jnp.bfloat16)
    return (grad_inner, jnp.sum(grad_inner.astype(jnp.float32), axis=0))


def back_input(grad_sum_two, grad_inner, kept_parts, params, mixers):
    hidden_mix, seq_mix = mixers
    mix_gain, weight_in = (params[0], params[2])
    normed_one, inverse_one = kept_parts[:2]
    seq_len, model_width = normed_one.shape
    grad_hidden = grad_sum_two + jnp.einsum(
        "lf,df->ld", grad_inner, weight_in, preferred_element_type=jnp.float32
    )
    mix_gain_grad = jnp.sum(grad_hidden * normed_one, axis=0)
    mix_bias_grad = jnp.sum(grad_hidden, axis=0)
    grad_mixed = norm_back(grad_hidden * mix_gain, normed_one, inverse_one)
    grad_seq = grad_mixed.astype(jnp.bfloat16)
    grad_spectra = jnp.einsum(
        "ml,md->ld", seq_mix, grad_seq, preferred_element_type=jnp.float32
    ).astype(jnp.bfloat16)
    grad_spectra = grad_spectra.reshape(2, seq_len, model_width)
    grad_in = grad_mixed + jnp.einsum(
        "kle,kde->ld", grad_spectra, hidden_mix, preferred_element_type=jnp.float32
    )
    return (grad_in, (mix_gain_grad, mix_bias_grad))


def exchange(block, distance):
    devices = range(lax.axis_size("dp"))
    return lax.ppermute(block, "dp", [(i, i ^ distance) for i in devices])


def add_low(first, second):
    return (first.astype(jnp.float32) + second.astype(jnp.float32)).astype(jnp.bfloat16)


def own_and_other(block, position):
    half = block.shape[0] // 2
    return (
        lax.dynamic_slice_in_dim(block, position * half, half),
        lax.dynamic_slice_in_dim(block, (1 - position) * half, half),
    )


def both_halves(own, other, position):
    return jnp.where(position == 0, jnp.concatenate([own, other]), jnp.concatenate([other, own]))


def sum_over_line(block):
    line = lax.axis_size("dp") // 4
    place = lax.axis_index("dp") // 4

    def along(value, steps):
        return lax.ppermute(
            value, "dp", [(a * 4 + j, b * 4 + j) for a, b in steps for j in range(4)]
        )

    if line == 4:
        block = add_low(block, along(block, [(0, 1), (3, 2)]))
        block = add_low(block, along(block, [(1, 2), (2, 1)]))
        spread = along(block, [(1, 0), (2, 3)])
        return jnp.where((place == 1) | (place == 2), block, spread)
    distance = 4
    while distance < 4 * line:
        block = add_low(block, exchange(block, distance))
        distance *= 2
    return block


def sum_chunk(block):
    place = lax.axis_index("dp")
    core, pair = (place % 2, (place // 2) % 2)
    own, other = own_and_other(block, core)
    chip_sum = add_low(own, exchange(other, 1))
    own, other = own_and_other(chip_sum, pair)
    pair_sum = add_low(own, exchange(other, 2))
    whole = sum_over_line(pair_sum)
    whole = both_halves(whole, exchange(whole, 2), pair)
    whole = both_halves(whole, exchange(whole, 1), core)
    return whole.astype(jnp.float32)


def sum_small(vectors):
    packed = jnp.concatenate(vectors)
    distance = 1
    while distance < lax.axis_size("dp"):
        packed = packed + exchange(packed, distance)
        distance *= 2
    return jnp.split(packed, np.cumsum([v.shape[0] for v in vectors])[:-1])


CHUNKS = 2


def per_device(
    activations,
    out_cotangent,
    doc_lengths,
    mix_gain,
    mix_bias,
    weight_in,
    bias_in,
    weight_out,
    bias_out,
    final_gain,
    final_bias,
):
    is_first = lax.axis_index("pipe") == 0
    row_count, seq_len, model_width = activations.shape
    params = (
        mix_gain[0],
        mix_bias[0],
        weight_in[0],
        bias_in[0],
        weight_out[0],
        bias_out[0],
        final_gain[0],
        final_bias[0],
    )
    cos_hid, sin_hid = dft_tables(model_width)
    cos_seq, sin_seq = dft_tables(seq_len)
    mixers = (
        jnp.asarray(np.stack([cos_hid, sin_hid]), jnp.bfloat16),
        jnp.asarray(np.concatenate([cos_seq, -sin_seq], axis=1), jnp.bfloat16),
    )
    padding = doc_lengths[:, -1]
    positions = jnp.arange(seq_len, dtype=jnp.int32)
    token_mask = (positions[None, :] < (seq_len - padding)[:, None]).astype(jnp.float32)

    def forward(row_in):
        result, kept_parts = forward_parts(row_in[None], params, mixers)
        return (result[0].astype(jnp.bfloat16), tuple(part[0] for part in kept_parts))

    def back_row(grad_out, kept_parts):
        grad_sum_two, grad_branch, out_terms = back_branch(grad_out, kept_parts, params)
        grad_inner, bias_in_grad = back_inner(grad_branch, kept_parts, params)
        grad_in, in_terms = back_input(grad_sum_two, grad_inner, kept_parts, params, mixers)
        terms = (*in_terms, bias_in_grad, *out_terms)
        return (grad_in, terms, (kept_parts[2], kept_parts[4], grad_branch, grad_inner))

    def only_if(condition, work, *operands):
        shapes = jax.eval_shape(work, *operands)
        blank = jax.tree.map(lambda s: jnp.zeros(s.shape, s.dtype), shapes)
        return lax.cond(condition, work, lambda *unused: blank, *operands)

    def later_row(row_in, row):
        result, kept_parts = forward(row_in)
        cotangent = out_cotangent[row].astype(jnp.float32) * token_mask[row][:, None]
        grad_in, terms, kept = back_row(cotangent, kept_parts)
        return (result, grad_in.astype(jnp.bfloat16), terms, kept)

    first_done = [only_if(is_first, forward, activations[row]) for row in range(row_count)]
    handed = [from_behind(done[0], "pipe", 1) for done in first_done]
    later_done = [
        only_if(~is_first, functools.partial(later_row, row=row), handed[row])
        for row in range(row_count)
    ]
    returned = [from_behind(done[1], "pipe", -1) for done in later_done]
    rows_done = []
    for row in range(row_count):

        def first_back(grad_low, kept_parts, unused_done):
            return back_row(grad_low.astype(jnp.float32), kept_parts)

        def pass_on(unused_grad, unused_parts, done):
            return (done[1].astype(jnp.float32), done[2], done[3])

        rows_done.append(
            lax.cond(
                is_first, first_back, pass_on, returned[row], first_done[row][1], later_done[row]
            )
        )
    layer_rows = jnp.stack(
        [
            jnp.where(is_first, first_done[row][0], later_done[row][0])
            for row in range(row_count)
        ]
    )
    grad_rows = jnp.stack([done[0] for done in rows_done])
    small = [sum(parts) for parts in zip(*[done[1] for done in rows_done])]
    hidden_low, active, grad_branch, grad_inner = (
        jnp.concatenate(parts) for parts in zip(*[done[2] for done in rows_done])
    )

    def summed(left, right):
        pieces = jnp.split(left, CHUNKS, axis=1)
        partial = [
            jnp.einsum("tf,td->fd", piece, right, preferred_element_type=jnp.float32)
            for piece in pieces
        ]
        return jnp.concatenate([sum_chunk(part.astype(jnp.bfloat16)) for part in partial])

    weight_out_grad = summed(active, grad_branch)
    weight_in_grad = summed(hidden_low, grad_inner)
    small = sum_small(small)
    return (
        layer_rows[None],
        grad_rows[None],
        small[0][None],
        small[1][None],
        weight_in_grad[None],
        small[2][None],
        weight_out_grad[None],
        small[3][None],
        small[4][None],
        small[5][None],
    )


def solution(mesh):
    placed = (
        P("dp", None, None),
        P("dp", None, None),
        P("dp", None),
        P("pipe", None),
        P("pipe", None),
        P("pipe", None, None),
        P("pipe", None),
        P("pipe", None, None),
        P("pipe", None),
        P("pipe", None),
        P("pipe", None),
    )
    return jax.shard_map(
        per_device,
        mesh=mesh,
        in_specs=placed,
        out_specs=(
            P("pipe", "dp", None, None),
            P("pipe", "dp", None, None),
            P("pipe", None),
            P("pipe", None),
            P("pipe", None, None),
            P("pipe", None),
            P("pipe", None, None),
            P("pipe", None),
            P("pipe", None),
            P("pipe", None),
        ),
        check_vma=False,
    )
```

time: 599 us -> 443 us (0.74)
  matrix products: 182 us -> 93.6 us
  waiting for transfers between devices: 257 us -> 171 us
  blocking collectives: 62 us -> 0 us
  local copies, waits for them, and re-layouts: 27.5 us -> 60.8 us
  starting transfers between devices: 13.3 us -> 46.1 us
  loops' own time: 0 us -> 18.4 us
  between operations: 15.8 us -> 2.03 us
  other arithmetic: 34 us -> 43.1 us
    psum x1 -> x0, waiting for transfers between devices: 233 us -> none  [per_device(): lax.psum((ordered[0], ordered[1], ordered[2], ordered[3], ordered[4], ord...]
    ppermute x0 -> x32, waiting for transfers between devices: none -> 120 us  [the longest x12 63.3 us: along(): lax.ppermute(value, 'dp', [(a * 4 + j, b * 4 + j) for a, b in steps for j...]
    psum x1 -> x0, blocking collectives: 62 us -> none  [per_device(): lax.psum((ordered[0], ordered[1], ordered[2], ordered[3], ordered[4], ord...]
    dot_general x18 -> x12, matrix products: 109 us -> 61 us  [the longest x2 19 us: back_inner(): jnp.einsum('ld,fd->lf', grad_branch, weight_out, preferred_element_type=j...]
    ppermute x0 -> x32, starting transfers between devices: none -> 39.1 us  [the longest x12 21.9 us: along(): lax.ppermute(value, 'dp', [(a * 4 + j, b * 4 + j) for a, b in steps for j...]
    ppermute x4, waiting for transfers between devices: 23.3 us -> 50.9 us  [from_behind(): return lax.ppermute(block, axis, route)]
    cond x0 -> x70, local copies, waits for them, and re-layouts: none -> 18.8 us
    another operation x0 -> x6, loops' own time: none -> 18.4 us  [the longest x4 17.8 us: only_if(): return lax.cond(condition, work, lambda *unused: blank, *operands)]
  transfers between devices with their start and end apart: 5 -> 36, of which waited for: 3 -> 13; matrix products, arithmetic and copies ran while one was open for 14% -> 26% of each run, Pallas kernels for 0% -> 0%
where the time goes in v1:
time: 443 us; the launch traced here: 435 us
  waiting for transfers between devices  171 us (39%)
  matrix products  93.6 us (21%)
  local copies, waits for them, and re-layouts  60.8 us (14%)
  starting transfers between devices  46.1 us (10%)
  other arithmetic  43.1 us (10%)
  loops' own time  18.4 us (4%)
    ppermute x12, waiting for transfers between devices, along(): lax.ppermute(value, 'dp', [(a * 4 + j, b * 4 + j) for a, b in steps for j...  63.3 us
    ppermute x20, waiting for transfers between devices, exchange(): return lax.ppermute(block, 'dp', [(i, i ^ distance) for i in devices])  56.3 us
    ppermute x4, waiting for transfers between devices, from_behind(): return lax.ppermute(block, axis, route)  50.9 us
    ppermute x12, starting transfers between devices, along(): lax.ppermute(value, 'dp', [(a * 4 + j, b * 4 + j) for a, b in steps for j...  21.9 us
    dot_general x2, matrix products, back_inner(): jnp.einsum('ld,fd->lf', grad_branch, weight_out, preferred_element_type=j...  19 us
    another operation x4, loops' own time, only_if(): return lax.cond(condition, work, lambda *unused: blank, *operands)  17.8 us
    ppermute x20, starting transfers between devices, exchange(): return lax.ppermute(block, 'dp', [(i, i ^ distance) for i in devices])  17.1 us
    another operation x24, local copies, waits for them, and re-layouts  15.7 us
  transfers between devices with their start and end apart: 36, of which 13 were waited for; matrix products, arithmetic and copies ran while one was open for 26% of the time, Pallas kernels for 0%

profile of v1, /device:TPU:0, one launch (start us, length us, event | category | flops | bytes accessed | tf_op | source)
XLA Modules:
  0.0 434.7 jit_solution(7828568444278303126)
XLA Ops:
  0.7 23.1 %conditional.6 = (bf16[512,768]{1,0:T(8,128)(2,1)S(1)}, f32[512,768]{1,0:T(8,128)}, f32[512,1]{0,1:T(1,128)S(1)}, bf16[512,768]{1,0:T(8,128)(2,1)}, f32[512,3072...) conditional(s32[]{:T(128)} %convert_element_type.389, () %tuple.60, ...), branch_computations={%region_0.0_spmd, %region_1.0_spmd} | conditional | flops 6871843840 | bytes 88776024 | solution.py:229
  4.2 3.4 convolution_convert_fusion
  10.6 6.4 %fusion.7 = (bf16[512,3072]{1,0:T(8,128)(2,1)}, f32[512,3072]{1,0:T(8,128)}) fusion(f32[3072]{0:T(1024)S(1)} %bitcast.368, bf16[512,768]{1,0:T(8,128)(2,1)S(1)} %get-tuple-element.710, bf16[768,3072]{1,0:T(8,128)(2,1)S(1)} %bitcast.339), kind=kOutput, calls=%fused_computation.10 | convolution fusion | flops 2431647744 | bytes 14954496 | tf_op jit(solution)/shard_map/cond/branch_1_fun/rld,df->rlf/dot_general | solution.py:57
  17.1 4.7 %fusion.137 = (f32[512]{0:T(512)S(1)}, f32[1,512,768]{2,1,0:T(8,128)S(1)}) fusion(f32[768]{0:T(1024)S(1)} %reduce.18, bf16[512,3072]{1,0:T(8,128)(2,1)} %get-tuple-element.712, bf16[3072,768]{1,0:T(8,128)(2,1)S(1)} %bitcast.361, f32[768]{0:T(1024)S(1)} %reduce.17, f32[768]{0:T(1024)S(1)} %reduce.16, f32[512]{0:T(512)S(1)} %add_rsqrt_fusion.1, ...), kind=kOutput, calls=%fused_computation.321 | convolution fusion | flops 2418671104 | bytes 11025408 | tf_op jit(solution)/shard_map/cond/branch_1_fun/rlf,fd->rld/dot_general | solution.py:62
  27.2 22.4 %conditional.8 = (bf16[512,768]{1,0:T(8,128)(2,1)}, f32[512,768]{1,0:T(8,128)}, f32[512,1]{0,1:T(1,128)S(1)}, bf16[512,768]{1,0:T(8,128)(2,1)}, f32[512,3072]{1,...) conditional(s32[]{:T(128)} %convert_element_type.389, () %tuple.64, ...), branch_computations={%region_22.23_spmd, %region_23.28_spmd} | conditional | flops 6871843840 | bytes 85581096 | solution.py:229
  27.6 3.4 convolution_convert_fusion.3
  34.2 7.9 %fusion.50 = (bf16[512,3072]{1,0:T(8,128)(2,1)}, f32[512,3072]{1,0:T(8,128)}) fusion(f32[3072]{0:T(1024)S(1)} %bitcast.369, bf16[512,768]{1,0:T(8,128)(2,1)} %get-tuple-element.670, bf16[768,3072]{1,0:T(8,128)(2,1)S(1)} %bitcast.341), kind=kOutput, calls=%fused_computation.99 | convolution fusion | flops 2431647744 | bytes 14954496 | tf_op jit(solution)/shard_map/cond/branch_1_fun/rld,df->rlf/dot_general | solution.py:57
  42.1 4.6 %fusion.139 = (f32[512]{0:T(512)S(1)}, f32[1,512,768]{2,1,0:T(8,128)S(1)}) fusion(f32[768]{0:T(1024)S(1)} %reduce.28, bf16[512,3072]{1,0:T(8,128)(2,1)} %get-tuple-element.672, bf16[3072,768]{1,0:T(8,128)(2,1)S(1)} %bitcast.363, f32[768]{0:T(1024)S(1)} %reduce.27, f32[768]{0:T(1024)S(1)} %reduce.26, f32[512]{0:T(512)S(1)} %add_rsqrt_fusion.5, ...), kind=kOutput, calls=%fused_computation.323 | convolution fusion | flops 2418671104 | bytes 11025408 | tf_op jit(solution)/shard_map/cond/branch_1_fun/rlf,fd->rld/dot_general | solution.py:62
  49.6 2.9 copy.72
  55.0 16.6 %conditional.7 = (bf16[512,768]{0,1:T(8,128)(2,1)}, f32[768]{0:T(1024)S(1)}, f32[768]{0:T(1024)S(1)}, f32[3072]{0:T(1024)S(1)}, f32[768]{0:T(1024)S(1)}, /*index...) conditional(s32[]{:T(128)} %convert_element_type.390, () %tuple.62, ...), branch_computations={%region_6.0_spmd, %region_7.22_spmd} | conditional | flops 13777102848 | bytes 187680224 | solution.py:229
  75.5 16.4 %conditional.9 = (bf16[512,768]{0,1:T(8,128)(2,1)}, f32[768]{0:T(1024)S(1)}, f32[768]{0:T(1024)S(1)}, f32[3072]{0:T(1024)S(1)}, f32[768]{0:T(1024)S(1)}, /*index...) conditional(s32[]{:T(128)} %convert_element_type.390, () %tuple.66, ...), branch_computations={%region_28.0_spmd, %region_29.0_spmd} | conditional | flops 13777102848 | bytes 187680224 | solution.py:229
  98.2 29.9 %collective-permute-done.2 = bf16[512,768]{1,0:T(8,128)(2,1)} collective-permute-done((bf16[512,768]{1,0:T(8,128)(2,1)}, bf16[512,768]{1,0:T(8,128)(2,1)}, u32[]{:S(2)}, u32[]{:S(2)}) %collective-permute-start.2) | collective-permute-done | bytes 786464 | tf_op jit(solution)/shard_map/ppermute | solution.py:17
  128.1 31.5 %conditional.10 = (f32[768]{0:T(1024)S(1)}, f32[768]{0:T(1024)S(1)}, f32[3072]{0:T(1024)S(1)}, f32[768]{0:T(1024)S(1)}, f32[768]{0:T(1024)S(1)}, /*index=5*/f32[...) conditional(s32[]{:T(128)} %convert_element_type.389, ...), branch_computations={%region_44.0_spmd, %region_45.0_spmd} | conditional | flops 6897394688 | bytes 107586848 | solution.py:254
  131.8 9.5 %convert_reduce_fusion.4 = (f32[3072]{0:T(1024)S(1)}, bf16[512,3072]{1,0:T(8,128)(2,1)}) fusion(f32[512,3072]{1,0:T(8,128)} %get-tuple-element.262, bf16[512,768]{1,0:T(8,128)(2,1)S(1)} %get-tuple-element.780, bf16[3072,768]{1,0:T(8,128)(2,1)S(1)} %copy-done.32), kind=kOutput, calls=%fused_computation.189 | convolution fusion | flops 2450519040 | bytes 14954496 | tf_op jit(solution)/shard_map/cond/branch_1_fun/ld,fd->lf/dot_general | solution.py:85
  141.3 5.8 %multiply_reduce_fusion.10 = (f32[512]{0:T(512)S(1)}, f32[768]{0:T(1024)S(1)}, f32[512]{0:T(512)S(1)}, f32[768]{0:T(1024)S(1)}, f32[512,768]{1,0:T(8,128)S(1)}) fusion(f32[512,768]{1,0:T(8,128)} %get-tuple-element.264, f32[768]{0:T(1024)S(1)} %reduce.37, bf16[512,3072]{1,0:T(8,128)(2,1)} %get-tuple-element.781, bf16[768,3072]{1,0:T(8,128)(2,1)S(1)} %bitcast.351, ...), kind=kOutput, calls=%fused_computation.204 | convolution fusion | flops 2421421568 | bytes 13391872 | tf_op jit(solution)/shard_map/cond/branch_1_fun/lf,df->ld/dot_general | solution.py:96
  151.7 4.0 fusion.100
  155.8 3.8 copy.225
  162.6 3.8 constant_dynamic-update-slice_fusion.4
  166.4 3.9 constant_dynamic-update-slice_fusion.6
  170.2 21.0 %collective-permute-done.3 = bf16[512,768]{1,0:T(8,128)(2,1)} collective-permute-done((bf16[512,768]{1,0:T(8,128)(2,1)}, bf16[512,768]{1,0:T(8,128)(2,1)}, u32[]{:S(2)}, u32[]{:S(2)}) %collective-permute-start.3) | collective-permute-done | bytes 786464 | tf_op jit(solution)/shard_map/ppermute | solution.py:17
  191.2 35.3 %conditional.11 = (f32[768]{0:T(1024)S(1)}, f32[768]{0:T(1024)S(1)}, f32[3072]{0:T(1024)S(1)}, f32[768]{0:T(1024)S(1)}, f32[768]{0:T(1024)S(1)}, /*index=5*/f32[...) conditional(s32[]{:T(128)} %convert_element_type.389, ...), branch_computations={%region_56.0_spmd, %region_57.0_spmd} | conditional | flops 6897394688 | bytes 107586848 | solution.py:254
  195.1 9.6 %convert_reduce_fusion.7 = (f32[3072]{0:T(1024)S(1)}, bf16[512,3072]{1,0:T(8,128)(2,1)}) fusion(f32[512,3072]{1,0:T(8,128)} %get-tuple-element.287, bf16[512,768]{1,0:T(8,128)(2,1)S(1)} %get-tuple-element.758, bf16[3072,768]{1,0:T(8,128)(2,1)S(1)} %copy-done.33), kind=kOutput, calls=%fused_computation.225 | convolution fusion | flops 2450519040 | bytes 14954496 | tf_op jit(solution)/shard_map/cond/branch_1_fun/ld,fd->lf/dot_general | solution.py:85
  204.6 5.8 %multiply_reduce_fusion.13 = (f32[512]{0:T(512)S(1)}, f32[768]{0:T(1024)S(1)}, f32[512]{0:T(512)S(1)}, f32[768]{0:T(1024)S(1)}, f32[512,768]{1,0:T(8,128)S(1)}) fusion(f32[512,768]{1,0:T(8,128)} %get-tuple-element.289, f32[768]{0:T(1024)S(1)} %reduce.39, bf16[512,3072]{1,0:T(8,128)(2,1)} %get-tuple-element.759, bf16[768,3072]{1,0:T(8,128)(2,1)S(1)} %bitcast.353, ...), kind=kOutput, calls=%fused_computation.240 | convolution fusion | flops 2421421568 | bytes 13391872 | tf_op jit(solution)/shard_map/cond/branch_1_fun/lf,df->ld/dot_general | solution.py:96
  211.7 3.9 fusion.119
  217.3 5.2 %fusion.118 = f32[1,512,768]{2,1,0:T(8,128)} fusion(bf16[2,512,768]{2,1,0:T(8,128)(2,1)S(1)} %bitcast.318, bf16[2,768,768]{2,1,0:T(8,128)(2,1)} %get-tuple-element.295, f32[512,768]{1,0:T(8,128)} %get-tuple-element.289, f32[512]{0:T(512)S(1)} %broadcast_multiply_fusion.20, f32[512]{0:T(512)S(1)} %broadcast_multiply_fusion.21, f32[512,768]{1,0:T(8,128)} %copy-done.48, ...), kind=kOutput, calls=%fused_computation.238 | convolution fusion | flops 1210318848 | bytes 8659968 | tf_op jit(solution)/shard_map/cond/branch_1_fun/kle,kde->ld/dot_general | solution.py:107
  222.5 3.9 copy.203
  229.0 6.0 %constant_dynamic-update-slice_fusion.3 = (bf16[1024,3072]{1,0:T(8,128)(2,1)}, bf16[1024,3072]{1,0:T(8,128)(2,1)}) fusion(bf16[1024,3072]{1,0:T(8,128)(2,1)} %constant_dynamic-update-slice_fusion.4, bf16[512,3072]{1,0:T(8,128)(2,1)} %get-tuple-element.425, bf16[1024,3072]{1,0:T(8,128)(2,1)} %constant_dynamic-update-slice_fusion.6, ...), kind=kLoop, calls=%fused_computation.299 | loop fusion | bytes 12582912 | tf_op jit(solution)/shard_map/concatenate | solution.py:267
  235.0 5.6 %convolution_convert_fusion.8 = bf16[384,3072]{1,0:T(8,128)(2,1)S(1)} fusion(bf16[1024,3072]{1,0:T(8,128)(2,1)} %get-tuple-element.657, bf16[1024,768]{1,0:T(8,128)(2,1)S(1)} %copy-done.21), kind=kOutput, calls=%fused_computation.256 | convolution fusion | flops 2417098752 | bytes 9437184 | tf_op jit(solution)/shard_map/tf,td->fd/dot_general | solution.py:273
  240.6 2.9 convolution_convert_fusion.9
  244.9 3.0 convolution_convert_fusion.10
  247.9 3.0 convolution_convert_fusion.11
  259.0 2.8 collective-permute-start.7
  261.8 3.3 maximum_bitcast_fusion.2
  271.6 10.8 %collective-permute-done.16 = bf16[96,3072]{1,0:T(8,128)(2,1)S(1)} collective-permute-done((bf16[96,3072]{1,0:T(8,128)(2,1)S(1)}, bf16[96,3072]{1,0:T(8,128)(2,1)S(1)}, u32[]{:S(2)}, u32[]{:S(2)}) %collective-permute-start.16) | collective-permute-done | bytes 589856 | tf_op jit(solution)/shard_map/ppermute | solution.py:115
  282.6 3.5 collective-permute-start.17
  286.1 9.0 %collective-permute-done.9 = bf16[96,3072]{1,0:T(8,128)(2,1)S(1)} collective-permute-done((bf16[96,3072]{1,0:T(8,128)(2,1)S(1)}, bf16[96,3072]{1,0:T(8,128)(2,1)S(1)}, u32[]{:S(2)}, u32[]{:S(2)}) %collective-permute-start.9) | collective-permute-done | bytes 589856 | tf_op jit(solution)/shard_map/ppermute | solution.py:115
  295.3 3.5 collective-permute-start.10
  298.8 9.0 %collective-permute-done.30 = bf16[384,768]{1,0:T(8,128)(2,1)S(1)} collective-permute-done((bf16[384,768]{1,0:T(8,128)(2,1)S(1)}, bf16[384,768]{1,0:T(8,128)(2,1)S(1)}, u32[]{:S(2)}, u32[]{:S(2)}) %collective-permute-start.30) | collective-permute-done | bytes 589856 | tf_op jit(solution)/shard_map/ppermute | solution.py:115
  307.9 3.5 collective-permute-start.31
  311.4 6.2 %collective-permute-done.23 = bf16[384,768]{1,0:T(8,128)(2,1)S(1)} collective-permute-done((bf16[384,768]{1,0:T(8,128)(2,1)S(1)}, bf16[384,768]{1,0:T(8,128)(2,1)S(1)}, u32[]{:S(2)}, u32[]{:S(2)}) %collective-permute-start.23) | collective-permute-done | bytes 589856 | tf_op jit(solution)/shard_map/ppermute | solution.py:115
  317.7 3.2 collective-permute-start.24
  323.8 7.6 %collective-permute-done.24 = bf16[384,768]{1,0:T(8,128)(2,1)S(1)} collective-permute-done((bf16[384,768]{1,0:T(8,128)(2,1)S(1)}, bf16[384,768]{1,0:T(8,128)(2,1)S(1)}, u32[]{:S(2)}, u32[]{:S(2)}) %collective-permute-start.24) | collective-permute-done | bytes 589856 | tf_op jit(solution)/shard_map/ppermute | solution.py:139
  338.1 41.5 %collective-permute-done.33 = bf16[384,768]{1,0:T(8,128)(2,1)S(1)} collective-permute-done((bf16[384,768]{1,0:T(8,128)(2,1)S(1)}, bf16[384,768]{1,0:T(8,128)(2,1)S(1)}, u32[]{:S(2)}, u32[]{:S(2)}) %collective-permute-start.33) | collective-permute-done | bytes 589856 | tf_op jit(solution)/shard_map/ppermute | solution.py:139
  381.9 14.2 %collective-permute-done.26 = bf16[384,768]{1,0:T(8,128)(2,1)S(1)} collective-permute-done((bf16[384,768]{1,0:T(8,128)(2,1)S(1)}, bf16[384,768]{1,0:T(8,128)(2,1)S(1)}, u32[]{:S(2)}, u32[]{:S(2)}) %collective-permute-start.26) | collective-permute-done | bytes 589856 | tf_op jit(solution)/shard_map/ppermute | solution.py:139
  398.9 15.2 %collective-permute-done.27 = bf16[384,768]{1,0:T(8,128)(2,1)S(1)} collective-permute-done((bf16[384,768]{1,0:T(8,128)(2,1)S(1)}, bf16[384,768]{1,0:T(8,128)(2,1)S(1)}, u32[]{:S(2)}, u32[]{:S(2)}) %collective-permute-start.27) | collective-permute-done | bytes 589856 | tf_op jit(solution)/shard_map/ppermute | solution.py:115
  418.4 2.8 collective-permute-done.13
  423.9 4.5 %fusion.123 = f32[1,3072,768]{2,1,0:T(8,128)} fusion(bf16[1536,768]{1,0:T(8,128)(2,1)S(1)} %maximum_select_fusion.3, bf16[1536,768]{1,0:T(8,128)(2,1)S(1)} %maximum_select_fusion.2), kind=kLoop, calls=%fused_computation.255 | loop fusion | flops 11796480 | bytes 14155776 | tf_op jit(solution)/shard_map/broadcast_in_dim | solution.py:288
  429.3 5.0 %fusion.122 = f32[1,768,3072]{2,1,0:T(8,128)} fusion(bf16[384,3072]{1,0:T(8,128)(2,1)S(1)} %maximum_select_fusion.1, bf16[384,3072]{1,0:T(8,128)(2,1)S(1)} %maximum_select_fusion), kind=kLoop, calls=%fused_computation.253 | loop fusion | flops 11796480 | bytes 14155776 | tf_op jit(solution)/shard_map/broadcast_in_dim | solution.py:286
  (295 shorter events, 104.9 us)
Async XLA Ops:
  9.1 8.0 %copy-start.28 = (f32[512]{0:T(512)}, f32[512]{0:T(512)S(1)}, u32[]{:S(2)}) copy-start(f32[512]{0:T(512)S(1)} %add_rsqrt_fusion.1) | copy-start | bytes 6148 | tf_op jit(solution)/shard_map/cond
  9.1 8.0 %slice-start.18 = ((s8[4718592]{0:T(1024)(128)(4,1)}), s8[4194304]{0:T(1024)(128)(4,1)S(1)}, s32[]{:S(2)}) async-start(s8[4718592]{0:T(1024)(128)(4,1)} %bitcast.360), calls=%async_computation.18 | async-start | bytes 8388608 | tf_op jit(solution)/shard_map/cond
  25.0 30.0 %collective-permute-start = (bf16[512,768]{0,1:T(8,128)(2,1)}, bf16[512,768]{0,1:T(8,128)(2,1)}, u32[]{:S(2)}, u32[]{:S(2)}) collective-permute-start(bf16[512,768]{0,1:T(8,128)(2,1)} %copy.69), channel_id=1, source_target_pairs={{0,16},{1,17},{2,18},{3,19},{4,20},{5,21},{6,22},{7,23},{8,24},{9,... | collective-permute-start | bytes 2359304 | tf_op jit(solution)/shard_map/ppermute | solution.py:17
  32.5 9.6 %copy-start.30 = (f32[512]{0:T(512)}, f32[512]{0:T(512)S(1)}, u32[]{:S(2)}) copy-start(f32[512]{0:T(512)S(1)} %add_rsqrt_fusion.5) | copy-start | bytes 6148 | tf_op jit(solution)/shard_map/cond
  32.5 9.6 %slice-start.20 = ((s8[4718592]{0:T(1024)(128)(4,1)}), s8[4194304]{0:T(1024)(128)(4,1)S(1)}, s32[]{:S(2)}) async-start(s8[4718592]{0:T(1024)(128)(4,1)} %bitcast.362), calls=%async_computation.20 | async-start | bytes 8388608 | tf_op jit(solution)/shard_map/cond
  52.5 23.0 %collective-permute-start.1 = (bf16[512,768]{0,1:T(8,128)(2,1)}, bf16[512,768]{0,1:T(8,128)(2,1)}, u32[]{:S(2)}, u32[]{:S(2)}) collective-permute-start(bf16[512,768]{0,1:T(8,128)(2,1)} %copy.72), channel_id=1, source_target_pairs={{0,16},{1,17},{2,18},{3,19},{4,20},{5,21},{6,22},{7,23},{8,24},{9,... | collective-permute-start | bytes 2359304 | tf_op jit(solution)/shard_map/ppermute | solution.py:17
  74.0 54.1 %collective-permute-start.2 = (bf16[512,768]{1,0:T(8,128)(2,1)}, bf16[512,768]{1,0:T(8,128)(2,1)}, u32[]{:S(2)}, u32[]{:S(2)}) collective-permute-start(bf16[512,768]{1,0:T(8,128)(2,1)} %copy.75), channel_id=1, source_target_pairs={{16,0},{17,1},{18,2},{19,3},{20,4},{21,5},{22,6},{23,7},{24,8},{25... | collective-permute-start | bytes 2359304 | tf_op jit(solution)/shard_map/ppermute | solution.py:17
  94.2 97.1 %collective-permute-start.3 = (bf16[512,768]{1,0:T(8,128)(2,1)}, bf16[512,768]{1,0:T(8,128)(2,1)}, u32[]{:S(2)}, u32[]{:S(2)}) collective-permute-start(bf16[512,768]{1,0:T(8,128)(2,1)} %copy.79), channel_id=1, source_target_pairs={{16,0},{17,1},{18,2},{19,3},{20,4},{21,5},{22,6},{23,7},{24,8},{25... | collective-permute-start | bytes 2359304 | tf_op jit(solution)/shard_map/ppermute | solution.py:17
  130.0 11.3 %slice-start.14 = ((s8[4718592]{0:T(1024)(128)(4,1)}), s8[4194304]{0:T(1024)(128)(4,1)S(1)}, s32[]{:S(2)}) async-start(s8[4718592]{0:T(1024)(128)(4,1)} %bitcast.350), calls=%async_computation.14 | async-start | bytes 8388608 | tf_op jit(solution)/shard_map/cond
  131.8 9.5 %copy-start.16 = (bf16[512,768]{1,0:T(8,128)(2,1)}, bf16[512,768]{1,0:T(8,128)(2,1)S(1)}, u32[]{:S(2)}) copy-start(bf16[512,768]{1,0:T(8,128)(2,1)S(1)} %get-tuple-element.780) | copy-start | bytes 2359300 | tf_op jit(solution)/shard_map/cond
  131.8 9.5 %slice-start.15 = ((s8[4718592]{0:T(1024)(128)(4,1)}), s8[524288]{0:T(1024)(128)(4,1)S(1)}, s32[]{:S(2)}) async-start(s8[4718592]{0:T(1024)(128)(4,1)} %bitcast.350), calls=%async_computation.15 | async-start | bytes 1048576 | tf_op jit(solution)/shard_map/cond
  166.4 24.8 %copy-start.1 = (f32[512,768]{1,0:T(8,128)S(1)}, f32[512,768]{1,0:T(8,128)}, u32[]{:S(2)}) copy-start(f32[512,768]{1,0:T(8,128)} %copy-done) | copy-start | bytes 4718596
  193.3 11.3 %slice-start.16 = ((s8[4718592]{0:T(1024)(128)(4,1)}), s8[4194304]{0:T(1024)(128)(4,1)S(1)}, s32[]{:S(2)}) async-start(s8[4718592]{0:T(1024)(128)(4,1)} %bitcast.352), calls=%async_computation.16 | async-start | bytes 8388608 | tf_op jit(solution)/shard_map/cond
  195.0 9.6 %copy-start.18 = (bf16[512,768]{1,0:T(8,128)(2,1)}, bf16[512,768]{1,0:T(8,128)(2,1)S(1)}, u32[]{:S(2)}) copy-start(bf16[512,768]{1,0:T(8,128)(2,1)S(1)} %get-tuple-element.758) | copy-start | bytes 2359300 | tf_op jit(solution)/shard_map/cond
  195.0 9.6 %slice-start.17 = ((s8[4718592]{0:T(1024)(128)(4,1)}), s8[524288]{0:T(1024)(128)(4,1)S(1)}, s32[]{:S(2)}) async-start(s8[4718592]{0:T(1024)(128)(4,1)} %bitcast.352), calls=%async_computation.17 | async-start | bytes 1048576 | tf_op jit(solution)/shard_map/cond
  235.0 9.3 %slice-start = ((s8[6291456]{0:T(1024)(128)(4,1)}), s8[4194304]{0:T(1024)(128)(4,1)S(1)}, s32[]{:S(2)}) async-start(s8[6291456]{0:T(1024)(128)(4,1)} %bitcast.313), calls=%async_computation | async-start | bytes 8388608
  243.6 7.5 %collective-permute-start.4 = (f32[6912]{0:T(1024)S(1)}, f32[6912]{0:T(1024)S(1)}, u32[]{:S(2)}, u32[]{:S(2)}) collective-permute-start(f32[6912]{0:T(1024)S(1)} %constant_dynamic-update-slice_fusion.9), channel_id=1, source_target_pairs={{0,1},{1,0},{2,3},{3,2},{4,5},{5,4},{6,7},{7,6},{8,9},{9,8},{10,11... | collective-permute-start | bytes 82952 | tf_op jit(solution)/shard_map/ppermute | solution.py:115
  243.8 21.9 %collective-permute-start.15 = (bf16[192,3072]{1,0:T(8,128)(2,1)S(1)}, bf16[192,3072]{1,0:T(8,128)(2,1)S(1)}, u32[]{:S(2)}, u32[]{:S(2)}) collective-permute-start(bf16[192,3072]{1,0:T(8,128)(2,1)S(1)} %constant_dynamic-slice_fusion.5), channel_id=1, source_target_pairs={{0,1},{1,0},{2,3},{3,2},{4,5},{5,4},{6,7},{7,6},{8,9},{9,8},{10,11... | collective-permute-start | bytes 3538952 | tf_op jit(solution)/shard_map/ppermute | solution.py:115
  251.0 16.7 %collective-permute-start.8 = (bf16[192,3072]{1,0:T(8,128)(2,1)S(1)}, bf16[192,3072]{1,0:T(8,128)(2,1)S(1)}, u32[]{:S(2)}, u32[]{:S(2)}) collective-permute-start(bf16[192,3072]{1,0:T(8,128)(2,1)S(1)} %constant_dynamic-slice_fusion.7), channel_id=1, source_target_pairs={{0,1},{1,0},{2,3},{3,2},{4,5},{5,4},{6,7},{7,6},{8,9},{9,8},{10,11... | collective-permute-start | bytes 3538952 | tf_op jit(solution)/shard_map/ppermute | solution.py:115
  251.1 3.9 collective-permute-start.5
  255.1 3.9 collective-permute-start.6
  257.0 11.8 %collective-permute-start.29 = (bf16[768,768]{1,0:T(8,128)(2,1)S(1)}, bf16[768,768]{1,0:T(8,128)(2,1)S(1)}, u32[]{:S(2)}, u32[]{:S(2)}) collective-permute-start(bf16[768,768]{1,0:T(8,128)(2,1)S(1)} %constant_dynamic-slice_fusion.1), channel_id=1, source_target_pairs={{0,1},{1,0},{2,3},{3,2},{4,5},{5,4},{6,7},{7,6},{8,9},{9,8},{10,11... | collective-permute-start | bytes 3538952 | tf_op jit(solution)/shard_map/ppermute | solution.py:115
  257.1 13.7 %collective-permute-start.22 = (bf16[768,768]{1,0:T(8,128)(2,1)S(1)}, bf16[768,768]{1,0:T(8,128)(2,1)S(1)}, u32[]{:S(2)}, u32[]{:S(2)}) collective-permute-start(bf16[768,768]{1,0:T(8,128)(2,1)S(1)} %constant_dynamic-slice_fusion.3), channel_id=1, source_target_pairs={{0,1},{1,0},{2,3},{3,2},{4,5},{5,4},{6,7},{7,6},{8,9},{9,8},{10,11... | collective-permute-start | bytes 3538952 | tf_op jit(solution)/shard_map/ppermute | solution.py:115
  259.0 6.1 %collective-permute-start.7 = (f32[6912]{0:T(1024)S(1)}, f32[6912]{0:T(1024)S(1)}, u32[]{:S(2)}, u32[]{:S(2)}) collective-permute-start(f32[6912]{0:T(1024)S(1)} %add.521), channel_id=1, source_target_pairs={{0,8},{1,9},{2,10},{3,11},{4,12},{5,13},{6,14},{7,15},{8,0},{9,1},... | collective-permute-start | bytes 82952 | tf_op jit(solution)/shard_map/ppermute | solution.py:115
  266.1 16.3 %collective-permute-start.16 = (bf16[96,3072]{1,0:T(8,128)(2,1)S(1)}, bf16[96,3072]{1,0:T(8,128)(2,1)S(1)}, u32[]{:S(2)}, u32[]{:S(2)}) collective-permute-start(bf16[96,3072]{1,0:T(8,128)(2,1)S(1)} %constant_dynamic-slice_fusion.4), channel_id=1, source_target_pairs={{0,2},{1,3},{2,0},{3,1},{4,6},{5,7},{6,4},{7,5},{8,10},{9,11},{10,... | collective-permute-start | bytes 1769480 | tf_op jit(solution)/shard_map/ppermute | solution.py:115
  268.2 26.9 %collective-permute-start.9 = (bf16[96,3072]{1,0:T(8,128)(2,1)S(1)}, bf16[96,3072]{1,0:T(8,128)(2,1)S(1)}, u32[]{:S(2)}, u32[]{:S(2)}) collective-permute-start(bf16[96,3072]{1,0:T(8,128)(2,1)S(1)} %constant_dynamic-slice_fusion.6), channel_id=1, source_target_pairs={{0,2},{1,3},{2,0},{3,1},{4,6},{5,7},{6,4},{7,5},{8,10},{9,11},{10,... | collective-permute-start | bytes 1769480 | tf_op jit(solution)/shard_map/ppermute | solution.py:115
  269.1 38.6 %collective-permute-start.30 = (bf16[384,768]{1,0:T(8,128)(2,1)S(1)}, bf16[384,768]{1,0:T(8,128)(2,1)S(1)}, u32[]{:S(2)}, u32[]{:S(2)}) collective-permute-start(bf16[384,768]{1,0:T(8,128)(2,1)S(1)} %constant_dynamic-slice_fusion), channel_id=1, source_target_pairs={{0,2},{1,3},{2,0},{3,1},{4,6},{5,7},{6,4},{7,5},{8,10},{9,11},{10,... | collective-permute-start | bytes 1769480 | tf_op jit(solution)/shard_map/ppermute | solution.py:115
  271.1 46.5 %collective-permute-start.23 = (bf16[384,768]{1,0:T(8,128)(2,1)S(1)}, bf16[384,768]{1,0:T(8,128)(2,1)S(1)}, u32[]{:S(2)}, u32[]{:S(2)}) collective-permute-start(bf16[384,768]{1,0:T(8,128)(2,1)S(1)} %constant_dynamic-slice_fusion.2), channel_id=1, source_target_pairs={{0,2},{1,3},{2,0},{3,1},{4,6},{5,7},{6,4},{7,5},{8,10},{9,11},{10,... | collective-permute-start | bytes 1769480 | tf_op jit(solution)/shard_map/ppermute | solution.py:115
  282.6 38.3 %collective-permute-start.17 = (bf16[96,3072]{1,0:T(8,128)(2,1)S(1)}, bf16[96,3072]{1,0:T(8,128)(2,1)S(1)}, u32[]{:S(2)}, u32[]{:S(2)}) collective-permute-start(bf16[96,3072]{1,0:T(8,128)(2,1)S(1)} %add_convert_fusion.16), channel_id=1, source_target_pairs={{0,4},{1,5},{2,6},{3,7},{12,8},{13,9},{14,10},{15,11},{16,20},{17,... | collective-permute-start | bytes 1769480 | tf_op jit(solution)/shard_map/ppermute | solution.py:139
  295.3 26.5 %collective-permute-start.10 = (bf16[96,3072]{1,0:T(8,128)(2,1)S(1)}, bf16[96,3072]{1,0:T(8,128)(2,1)S(1)}, u32[]{:S(2)}, u32[]{:S(2)}) collective-permute-start(bf16[96,3072]{1,0:T(8,128)(2,1)S(1)} %add_convert_fusion.19), channel_id=1, source_target_pairs={{0,4},{1,5},{2,6},{3,7},{12,8},{13,9},{14,10},{15,11},{16,20},{17,... | collective-permute-start | bytes 1769480 | tf_op jit(solution)/shard_map/ppermute | solution.py:139
  307.9 15.0 %collective-permute-start.31 = (bf16[384,768]{1,0:T(8,128)(2,1)S(1)}, bf16[384,768]{1,0:T(8,128)(2,1)S(1)}, u32[]{:S(2)}, u32[]{:S(2)}) collective-permute-start(bf16[384,768]{1,0:T(8,128)(2,1)S(1)} %add_convert_fusion.10), channel_id=1, source_target_pairs={{0,4},{1,5},{2,6},{3,7},{12,8},{13,9},{14,10},{15,11},{16,20},{17,... | collective-permute-start | bytes 1769480 | tf_op jit(solution)/shard_map/ppermute | solution.py:139
  317.7 13.7 %collective-permute-start.24 = (bf16[384,768]{1,0:T(8,128)(2,1)S(1)}, bf16[384,768]{1,0:T(8,128)(2,1)S(1)}, u32[]{:S(2)}, u32[]{:S(2)}) collective-permute-start(bf16[384,768]{1,0:T(8,128)(2,1)S(1)} %add_convert_fusion.13), channel_id=1, source_target_pairs={{0,4},{1,5},{2,6},{3,7},{12,8},{13,9},{14,10},{15,11},{16,20},{17,... | collective-permute-start | bytes 1769480 | tf_op jit(solution)/shard_map/ppermute | solution.py:139
  321.1 11.2 %collective-permute-start.18 = (bf16[96,3072]{1,0:T(8,128)(2,1)S(1)}, bf16[96,3072]{1,0:T(8,128)(2,1)S(1)}, u32[]{:S(2)}, u32[]{:S(2)}) collective-permute-start(bf16[96,3072]{1,0:T(8,128)(2,1)S(1)} %add_convert_fusion.15), channel_id=1, source_target_pairs={{4,8},{5,9},{6,10},{7,11},{8,4},{9,5},{10,6},{11,7},{20,24},{21,25... | collective-permute-start | bytes 1769480 | tf_op jit(solution)/shard_map/ppermute | solution.py:139
  322.0 13.2 %collective-permute-start.11 = (bf16[96,3072]{1,0:T(8,128)(2,1)S(1)}, bf16[96,3072]{1,0:T(8,128)(2,1)S(1)}, u32[]{:S(2)}, u32[]{:S(2)}) collective-permute-start(bf16[96,3072]{1,0:T(8,128)(2,1)S(1)} %add_convert_fusion.18), channel_id=1, source_target_pairs={{4,8},{5,9},{6,10},{7,11},{8,4},{9,5},{10,6},{11,7},{20,24},{21,25... | collective-permute-start | bytes 1769480 | tf_op jit(solution)/shard_map/ppermute | solution.py:139
  323.1 10.6 %collective-permute-start.32 = (bf16[384,768]{1,0:T(8,128)(2,1)S(1)}, bf16[384,768]{1,0:T(8,128)(2,1)S(1)}, u32[]{:S(2)}, u32[]{:S(2)}) collective-permute-start(bf16[384,768]{1,0:T(8,128)(2,1)S(1)} %add_convert_fusion.9), channel_id=1, source_target_pairs={{4,8},{5,9},{6,10},{7,11},{8,4},{9,5},{10,6},{11,7},{20,24},{21,25... | collective-permute-start | bytes 1769480 | tf_op jit(solution)/shard_map/ppermute | solution.py:139
  331.6 5.1 %collective-permute-start.25 = (bf16[384,768]{1,0:T(8,128)(2,1)S(1)}, bf16[384,768]{1,0:T(8,128)(2,1)S(1)}, u32[]{:S(2)}, u32[]{:S(2)}) collective-permute-start(bf16[384,768]{1,0:T(8,128)(2,1)S(1)} %add_convert_fusion.12), channel_id=1, source_target_pairs={{4,8},{5,9},{6,10},{7,11},{8,4},{9,5},{10,6},{11,7},{20,24},{21,25... | collective-permute-start | bytes 1769480 | tf_op jit(solution)/shard_map/ppermute | solution.py:139
  332.4 48.8 %collective-permute-start.19 = (bf16[96,3072]{1,0:T(8,128)(2,1)S(1)}, bf16[96,3072]{1,0:T(8,128)(2,1)S(1)}, u32[]{:S(2)}, u32[]{:S(2)}) collective-permute-start(bf16[96,3072]{1,0:T(8,128)(2,1)S(1)} %add_convert_fusion.14), channel_id=1, source_target_pairs={{4,0},{5,1},{6,2},{7,3},{8,12},{9,13},{10,14},{11,15},{20,16},{21,... | collective-permute-start | bytes 1769480 | tf_op jit(solution)/shard_map/ppermute | solution.py:139
  333.9 45.7 %collective-permute-start.33 = (bf16[384,768]{1,0:T(8,128)(2,1)S(1)}, bf16[384,768]{1,0:T(8,128)(2,1)S(1)}, u32[]{:S(2)}, u32[]{:S(2)}) collective-permute-start(bf16[384,768]{1,0:T(8,128)(2,1)S(1)} %add_convert_fusion.8), channel_id=1, source_target_pairs={{4,0},{5,1},{6,2},{7,3},{8,12},{9,13},{10,14},{11,15},{20,16},{21,... | collective-permute-start | bytes 1769480 | tf_op jit(solution)/shard_map/ppermute | solution.py:139
  335.3 63.0 %collective-permute-start.12 = (bf16[96,3072]{1,0:T(8,128)(2,1)S(1)}, bf16[96,3072]{1,0:T(8,128)(2,1)S(1)}, u32[]{:S(2)}, u32[]{:S(2)}) collective-permute-start(bf16[96,3072]{1,0:T(8,128)(2,1)S(1)} %add_convert_fusion.17), channel_id=1, source_target_pairs={{4,0},{5,1},{6,2},{7,3},{8,12},{9,13},{10,14},{11,15},{20,16},{21,... | collective-permute-start | bytes 1769480 | tf_op jit(solution)/shard_map/ppermute | solution.py:139
  336.8 59.3 %collective-permute-start.26 = (bf16[384,768]{1,0:T(8,128)(2,1)S(1)}, bf16[384,768]{1,0:T(8,128)(2,1)S(1)}, u32[]{:S(2)}, u32[]{:S(2)}) collective-permute-start(bf16[384,768]{1,0:T(8,128)(2,1)S(1)} %add_convert_fusion.11), channel_id=1, source_target_pairs={{4,0},{5,1},{6,2},{7,3},{8,12},{9,13},{10,14},{11,15},{20,16},{21,... | collective-permute-start | bytes 1769480 | tf_op jit(solution)/shard_map/ppermute | solution.py:139
  379.6 18.1 %collective-permute-start.34 = (bf16[384,768]{1,0:T(8,128)(2,1)S(1)}, bf16[384,768]{1,0:T(8,128)(2,1)S(1)}, u32[]{:S(2)}, u32[]{:S(2)}) collective-permute-start(bf16[384,768]{1,0:T(8,128)(2,1)S(1)} %broadcast_select_fusion), channel_id=1, source_target_pairs={{0,2},{1,3},{2,0},{3,1},{4,6},{5,7},{6,4},{7,5},{8,10},{9,11},{10,... | collective-permute-start | bytes 1769480 | tf_op jit(solution)/shard_map/ppermute | solution.py:115
  381.3 33.4 %collective-permute-start.20 = (bf16[96,3072]{1,0:T(8,128)(2,1)S(1)}, bf16[96,3072]{1,0:T(8,128)(2,1)S(1)}, u32[]{:S(2)}, u32[]{:S(2)}) collective-permute-start(bf16[96,3072]{1,0:T(8,128)(2,1)S(1)} %broadcast_select_fusion.2), channel_id=1, source_target_pairs={{0,2},{1,3},{2,0},{3,1},{4,6},{5,7},{6,4},{7,5},{8,10},{9,11},{10,... | collective-permute-start | bytes 1769480 | tf_op jit(solution)/shard_map/ppermute | solution.py:115
  396.2 18.0 %collective-permute-start.27 = (bf16[384,768]{1,0:T(8,128)(2,1)S(1)}, bf16[384,768]{1,0:T(8,128)(2,1)S(1)}, u32[]{:S(2)}, u32[]{:S(2)}) collective-permute-start(bf16[384,768]{1,0:T(8,128)(2,1)S(1)} %broadcast_select_fusion.1), channel_id=1, source_target_pairs={{0,2},{1,3},{2,0},{3,1},{4,6},{5,7},{6,4},{7,5},{8,10},{9,11},{10,... | collective-permute-start | bytes 1769480 | tf_op jit(solution)/shard_map/ppermute | solution.py:115
  398.2 23.3 %collective-permute-start.35 = (bf16[768,768]{1,0:T(8,128)(2,1)S(1)}, bf16[768,768]{1,0:T(8,128)(2,1)S(1)}, u32[]{:S(2)}, u32[]{:S(2)}) collective-permute-start(bf16[768,768]{1,0:T(8,128)(2,1)S(1)} %maximum_select_fusion.7), channel_id=1, source_target_pairs={{0,1},{1,0},{2,3},{3,2},{4,5},{5,4},{6,7},{7,6},{8,9},{9,8},{10,11... | collective-permute-start | bytes 3538952 | tf_op jit(solution)/shard_map/ppermute | solution.py:115
  398.4 22.8 %collective-permute-start.13 = (bf16[96,3072]{1,0:T(8,128)(2,1)S(1)}, bf16[96,3072]{1,0:T(8,128)(2,1)S(1)}, u32[]{:S(2)}, u32[]{:S(2)}) collective-permute-start(bf16[96,3072]{1,0:T(8,128)(2,1)S(1)} %broadcast_select_fusion.3), channel_id=1, source_target_pairs={{0,2},{1,3},{2,0},{3,1},{4,6},{5,7},{6,4},{7,5},{8,10},{9,11},{10,... | collective-permute-start | bytes 1769480 | tf_op jit(solution)/shard_map/ppermute | solution.py:115
  414.6 7.5 %collective-permute-start.28 = (bf16[768,768]{1,0:T(8,128)(2,1)S(1)}, bf16[768,768]{1,0:T(8,128)(2,1)S(1)}, u32[]{:S(2)}, u32[]{:S(2)}) collective-permute-start(bf16[768,768]{1,0:T(8,128)(2,1)S(1)} %maximum_select_fusion.6), channel_id=1, source_target_pairs={{0,1},{1,0},{2,3},{3,2},{4,5},{5,4},{6,7},{7,6},{8,9},{9,8},{10,11... | collective-permute-start | bytes 3538952 | tf_op jit(solution)/shard_map/ppermute | solution.py:115
  415.0 8.0 %collective-permute-start.21 = (bf16[192,3072]{1,0:T(8,128)(2,1)S(1)}, bf16[192,3072]{1,0:T(8,128)(2,1)S(1)}, u32[]{:S(2)}, u32[]{:S(2)}) collective-permute-start(bf16[192,3072]{1,0:T(8,128)(2,1)S(1)} %maximum_select_fusion.5), channel_id=1, source_target_pairs={{0,1},{1,0},{2,3},{3,2},{4,5},{5,4},{6,7},{7,6},{8,9},{9,8},{10,11... | collective-permute-start | bytes 3538952 | tf_op jit(solution)/shard_map/ppermute | solution.py:115
  421.4 6.9 %collective-permute-start.14 = (bf16[192,3072]{1,0:T(8,128)(2,1)S(1)}, bf16[192,3072]{1,0:T(8,128)(2,1)S(1)}, u32[]{:S(2)}, u32[]{:S(2)}) collective-permute-start(bf16[192,3072]{1,0:T(8,128)(2,1)S(1)} %maximum_select_fusion.4), channel_id=1, source_target_pairs={{0,1},{1,0},{2,3},{3,2},{4,5},{5,4},{6,7},{7,6},{8,9},{9,8},{10,11... | collective-permute-start | bytes 3538952 | tf_op jit(solution)/shard_map/ppermute | solution.py:115
  (37 other events, 147.5 us)
